TPU v7x, 256 devices: a whole 4x4x8 slice. The times are simulated.
256 devices in a mesh: gx: 32 (over z, y), gy: 8 (over x, core).
Axes of the slice: x: 4, y: 4, z: 8, core: 2. Of those that a mesh axis runs over, the one named last changes fastest.
Arguments:
- load_vector: float32 [64, 16, 192, 128], P('gx', 'gy'), may hold values from -6 to 6
- blocks: bfloat16 [4, 64, 16, 192, 192], P(None, 'gx', 'gy'), may hold values from -11 to 13
Outputs:
- solution: float32 [64, 16, 192, 128], P('gx', 'gy')
All inputs are finite; a program needn't handle non-finite values.
Results may differ from a plain program's by a relative error of at most 0.0038.
Values may be sent and summed in bfloat16 or wider, within the bound.
A program may use at most 64 MiB of HBM per device.

v0:
```python
import jax
import jax.numpy as jnp
from jax import lax
from jax.sharding import PartitionSpec as P

OV = 1
ITERS = 2


def extended(block, sides, width):
    for axis, dim in sides:
        count = lax.axis_size(axis)
        forward = [(i, i + 1) for i in range(count - 1)]
        backward = [(target, source) for source, target in forward]
        low = lax.ppermute(
            lax.slice_in_dim(block, block.shape[dim] - width, None, axis=dim), axis, forward
        )
        high = lax.ppermute(lax.slice_in_dim(block, 0, width, axis=dim), axis, backward)
        block = jnp.concatenate([low, block, high], axis=dim)
    return block


def local_product(matrices, operand):
    return jnp.einsum("xyij,xyjr->xyir", matrices, operand, preferred_element_type=jnp.float32)


def local_transposed(matrices, operand):
    return jnp.einsum("xyji,xyjr->xyir", matrices, operand, preferred_element_type=jnp.float32)


def couple_box(blocks, operand):
    total = local_product(blocks[0], operand)
    total = total + local_product(blocks[1], jnp.pad(operand[1:], ((0, 1), (0, 0), (0, 0), (0, 0))))
    total = total + jnp.pad(
        local_transposed(blocks[1], operand)[:-1], ((1, 0), (0, 0), (0, 0), (0, 0))
    )
    total = total + local_product(
        blocks[2], jnp.pad(operand[:, 1:], ((0, 0), (0, 1), (0, 0), (0, 0)))
    )
    total = total + jnp.pad(
        local_transposed(blocks[2], operand)[:, :-1], ((0, 0), (1, 0), (0, 0), (0, 0))
    )
    return total


def couple_inner(blocks, operand):
    total = local_product(blocks[0, 1:-1, 1:-1], operand[1:-1, 1:-1])
    total = total + local_product(blocks[1, 1:-1, 1:-1], operand[2:, 1:-1])
    total = total + local_transposed(blocks[1, :-2, 1:-1], operand[:-2, 1:-1])
    total = total + local_product(blocks[2, 1:-1, 1:-1], operand[1:-1, 2:])
    total = total + local_transposed(blocks[2, 1:-1, :-2], operand[1:-1, :-2])
    return total


def smooth_box(blocks, values):
    smoothed = local_product(blocks[3], values.astype(jnp.bfloat16))
    defect = values - couple_box(blocks, smoothed.astype(jnp.bfloat16))
    smoothed = smoothed + local_product(blocks[3], defect.astype(jnp.bfloat16))
    return smoothed


def owned_part(vector, rows_first, rows_second, margin):
    return vector[margin : margin + rows_first, margin : margin + rows_second]


def rotate_solve(columns, initial_norm):
    column_count = len(columns)
    targets = [initial_norm] + [jnp.zeros_like(initial_norm) for position in range(column_count)]
    cosines = []
    sine_list = []
    triangle = []
    for column_index in range(column_count):
        entries = list(columns[column_index])
        for earlier in range(column_index):
            upper_entry = (
                cosines[earlier] * entries[earlier] + sine_list[earlier] * entries[earlier + 1]
            )
            lower_entry = (
                cosines[earlier] * entries[earlier + 1] - sine_list[earlier] * entries[earlier]
            )
            entries[earlier] = upper_entry
            entries[earlier + 1] = lower_entry
        radius = jnp.sqrt(
            entries[column_index] * entries[column_index]
            + entries[column_index + 1] * entries[column_index + 1]
        )
        cosine = entries[column_index] / radius
        sine = entries[column_index + 1] / radius
        entries[column_index] = radius
        cosines.append(cosine)
        sine_list.append(sine)
        lower_target = -sine * targets[column_index]
        targets[column_index] = cosine * targets[column_index]
        targets[column_index + 1] = lower_target
        triangle.append(entries[: column_index + 1])
    weights = [None] * column_count
    for column_index in reversed(range(column_count)):
        running = targets[column_index]
        for later in range(column_index + 1, column_count):
            running = running - triangle[later][column_index] * weights[later]
        weights[column_index] = running / triangle[column_index][column_index]
    return weights


def local(load_vector, blocks):
    rows_first = load_vector.shape[0]
    rows_second = load_vector.shape[1]
    total_square = lax.psum(jnp.sum(load_vector * load_vector, axis=(0, 1, 2)), ("gx", "gy"))
    initial_norm = jnp.sqrt(total_square)
    first_vector = load_vector / initial_norm
    near_blocks = extended(blocks, (("gx", 1), ("gy", 2)), OV)
    krylov_basis = [first_vector]
    margin = 0
    corrections = []
    columns = []
    for iteration in range(ITERS):
        boxed = extended(krylov_basis[iteration], (("gx", 0), ("gy", 1)), OV)
        correction = owned_part(smooth_box(near_blocks, boxed), rows_first, rows_second, OV)
        corrections.append(correction)
        rounded = correction.astype(jnp.bfloat16)
        bordered = extended(rounded, (("gx", 0), ("gy", 1)), 1)
        product_vector = couple_inner(near_blocks, bordered)
        owned_product = owned_part(product_vector, rows_first, rows_second, margin)
        partial_value = jnp.stack(
            [
                jnp.sum(
                    owned_part(vector, rows_first, rows_second, margin) * owned_product,
                    axis=(0, 1, 2),
                )
                for vector in krylov_basis
            ]
        )
        heights = lax.psum(partial_value, ("gx", "gy"))
        for position in range(len(krylov_basis)):
            product_vector = product_vector - heights[position] * krylov_basis[position]
        projected = owned_part(product_vector, rows_first, rows_second, margin)
        subdiagonal = jnp.sqrt(
            lax.psum(jnp.sum(projected * projected, axis=(0, 1, 2)), ("gx", "gy"))
        )
        columns.append([heights[position] for position in range(len(krylov_basis))] + [subdiagonal])
        if iteration + 1 < ITERS:
            krylov_basis.append(product_vector / subdiagonal)
    weights = rotate_solve(columns, initial_norm)
    solution = weights[0] * corrections[0]
    position = 1
    solution = solution + weights[position] * corrections[position]
    return solution


def solution(mesh):
    return jax.shard_map(
        local,
        mesh=mesh,
        in_specs=(P("gx", "gy", None, None), P(None, "gx", "gy", None, None)),
        out_specs=P("gx", "gy", None, None),
        check_vma=False,
    )
```

profile of v0, /device:TPU:1, one launch (start us, length us, event | category | flops | bytes accessed | tf_op | source)
XLA Modules:
  0.0 548.8 jit_solution(844993674247347810)
XLA Ops:
  0.0 2.4 fusion.79
  2.4 5.0 collective-permute-start
  8.8 91.5 %psum.35 = f32[128]{0:T(128)S(1)} all-reduce(f32[128]{0:T(128)S(1)} %multiply_reduce_fusion.5), channel_id=1, replica_groups=mesh['gx'=32,'gy'=8] {'gx','gy'}, use_global_device_ids=true, to_apply=%region_1.0 | all-reduce | flops 128 | bytes 1024 | tf_op jit(solution)/shard_map/psum | solution.py:108
  101.6 1.5 constant_dynamic-update-slice_fusion.1
  104.3 1.8 fusion.78
  106.1 2.6 collective-permute-start.3
  108.7 3.0 collective-permute-start.2
  112.5 3.4 collective-permute-start.4
  117.2 2.7 copy.4
  120.0 3.7 collective-permute-done.5
  125.7 3.6 collective-permute-start.6
  129.3 2.1 collective-permute-start.7
  131.4 2.4 copy.3
  133.9 1.8 fusion.29
  135.7 3.2 pad_maximum_fusion
  139.0 4.1 fusion.88
  143.9 1.6 fusion.19
  145.6 1.7 fusion.16
  147.2 1.7 fusion.1
  149.0 1.8 fusion.17
  150.7 6.1 %fusion.2 = f32[4,4,192,128]{3,2,1,0:T(8,128)} fusion(f32[4,3,192,128]{3,2,1,0:T(8,128)} %fusion.19, f32[3,4,192,128]{3,2,1,0:T(8,128)} %fusion.16, f32[4,4,192,128]{3,2,1,0:T(8,128)} %fusion.1, f32[4,4,192,128]{3,2,1,0:T(8,128)} %fusion.17, bf16[4,4,4,192,192]{4,3,2,1,0:T(8,128)(2,1)} %copy-done, bf16[4,3,192,128]{3,2,1,0:T(8,128)(2,1)} %slice.234, ...), kind=kOutput, calls=%fused_computation.11 | convolution fusion | flops 305922048 | bytes 12386304 | tf_op jit(solution)/shard_map/xyij,xyjr->xyir/dot_general | solution.py:24
  159.3 1.9 collective-permute-start.9
  161.2 1.3 collective-permute-start.8
  163.7 4.3 collective-permute-done.8
  168.2 2.0 collective-permute-start.10
  170.1 4.3 collective-permute-start.11
  177.8 82.2 %psum.36 = f32[128]{0:T(128)S(1)} all-reduce(f32[128]{0:T(128)S(1)} %get-tuple-element.33), channel_id=1, replica_groups=mesh['gx'=32,'gy'=8] {'gx','gy'}, use_global_device_ids=true, to_apply=%region_3.4 | all-reduce | flops 128 | bytes 1024 | tf_op jit(solution)/shard_map/psum | solution.py:133
  260.1 72.7 %psum.37 = f32[128]{0:T(128)S(1)} all-reduce(f32[128]{0:T(128)S(1)} %multiply_reduce_fusion.3), channel_id=1, replica_groups=mesh['gx'=32,'gy'=8] {'gx','gy'}, use_global_device_ids=true, to_apply=%region_5.6 | all-reduce | flops 128 | bytes 1024 | tf_op jit(solution)/shard_map/psum | solution.py:138
  332.9 2.8 collective-permute-start.12
  337.0 2.2 collective-permute-done.12
  339.2 3.8 collective-permute-done.13
  343.1 3.4 collective-permute-start.14
  346.5 2.3 collective-permute-start.15
  348.8 2.4 collective-permute-done.14
  351.2 4.5 collective-permute-done.15
  355.8 3.3 fusion.89
  359.2 1.6 fusion.18
  360.8 1.7 fusion.14
  362.5 1.8 fusion
  364.3 1.7 fusion.15
  366.0 5.9 %fusion.3 = f32[4,4,192,128]{3,2,1,0:T(8,128)} fusion(f32[4,3,192,128]{3,2,1,0:T(8,128)} %fusion.18, f32[3,4,192,128]{3,2,1,0:T(8,128)} %fusion.14, f32[4,4,192,128]{3,2,1,0:T(8,128)} %fusion, f32[4,4,192,128]{3,2,1,0:T(8,128)} %fusion.15, bf16[4,4,4,192,192]{4,3,2,1,0:T(8,128)(2,1)} %copy-done, bf16[4,3,192,128]{3,2,1,0:T(8,128)(2,1)S(1)} %slice.246, ...), kind=kOutput, calls=%fused_computation.12 | convolution fusion | flops 305922048 | bytes 12386304 | tf_op jit(solution)/shard_map/xyij,xyjr->xyir/dot_general | solution.py:24
  373.1 3.4 collective-permute-start.17
  378.2 5.1 collective-permute-done.16
  383.4 2.1 collective-permute-start.18
  385.4 3.6 collective-permute-start.19
  392.3 80.8 %psum.38 = f32[2,128]{1,0:T(2,128)S(1)} all-reduce(f32[2,128]{1,0:T(2,128)S(1)} %pad_maximum_fusion.45), channel_id=1, replica_groups=mesh['gx'=32,'gy'=8] {'gx','gy'}, use_global_device_ids=true, to_apply=%region_8.9 | all-reduce | flops 256 | bytes 2048 | tf_op jit(solution)/shard_map/psum | solution.py:133
  473.2 73.4 %psum.39 = f32[128]{0:T(128)S(1)} all-reduce(f32[128]{0:T(128)S(1)} %multiply_reduce_fusion), channel_id=1, replica_groups=mesh['gx'=32,'gy'=8] {'gx','gy'}, use_global_device_ids=true, to_apply=%region_10.11 | all-reduce | flops 128 | bytes 1024 | tf_op jit(solution)/shard_map/psum | solution.py:138
  546.6 2.2 multiply_add_fusion
  (87 shorter events, 23.7 us)
Async XLA Ops:
  0.0 8.7 %copy-start.2 = (f32[2,2,192,128]{3,2,1,0:T(8,128)S(1)}, f32[2,2,192,128]{3,2,1,0:T(8,128)}, u32[]{:S(2)}) copy-start(f32[2,2,192,128]{3,2,1,0:T(8,128)} %param.2) | copy-start | bytes 1179652
  2.4 97.9 %collective-permute-start = (bf16[4,1,2,192,192]{4,3,2,1,0:T(8,128)(2,1)S(1)}, bf16[4,1,2,192,192]{4,3,2,1,0:T(8,128)(2,1)}, u32[]{:S(2)}, u32[]{:S(2)}) collective-permute-start(bf16[4,1,2,192,192]{4,3,2,1,0:T(8,128)(2,1)S(1)} %get-tuple-element.12), channel_id=1, source_target_pairs={{0,8},{8,16},{16,24},{24,32},{32,40},{40,48},{48,56},{56,64},{64,7... | collective-permute-start | bytes 1769480 | tf_op jit(solution)/shard_map/ppermute | solution.py:15
  7.4 95.7 %collective-permute-start.1 = (bf16[4,1,2,192,192]{4,3,2,1,0:T(8,128)(2,1)}, bf16[4,1,2,192,192]{4,3,2,1,0:T(8,128)(2,1)}, u32[]{:S(2)}, u32[]{:S(2)}) collective-permute-start(bf16[4,1,2,192,192]{4,3,2,1,0:T(8,128)(2,1)} %get-tuple-element.11), channel_id=1, source_target_pairs={{8,0},{16,8},{24,16},{32,24},{40,32},{48,40},{56,48},{64,56},{72,6... | collective-permute-start | bytes 1769480 | tf_op jit(solution)/shard_map/ppermute | solution.py:18
  104.3 7.4 %copy-start.3 = (f32[2,2,192,128]{3,2,1,0:T(8,128)S(1)}, f32[2,2,192,128]{3,2,1,0:T(8,128)}, u32[]{:S(2)}) copy-start(f32[2,2,192,128]{3,2,1,0:T(8,128)} %param.2) | copy-start | bytes 1179652
  106.1 29.5 %collective-permute-start.3 = (bf16[4,4,1,192,192]{4,3,2,1,0:T(8,128)(2,1)}, bf16[4,4,1,192,192]{4,3,2,1,0:T(8,128)(2,1)}, u32[]{:S(2)}, u32[]{:S(2)}) collective-permute-start(bf16[4,4,1,192,192]{4,3,2,1,0:T(8,128)(2,1)} %get-tuple-element.9), channel_id=1, source_target_pairs={{1,0},{2,1},{3,2},{4,3},{5,4},{6,5},{7,6},{9,8},{10,9},{11,10},{12... | collective-permute-start | bytes 3538952 | tf_op jit(solution)/shard_map/ppermute | solution.py:18
  108.7 27.0 %collective-permute-start.2 = (bf16[4,4,1,192,192]{4,3,2,1,0:T(8,128)(2,1)}, bf16[4,4,1,192,192]{4,3,2,1,0:T(8,128)(2,1)}, u32[]{:S(2)}, u32[]{:S(2)}) collective-permute-start(bf16[4,4,1,192,192]{4,3,2,1,0:T(8,128)(2,1)} %get-tuple-element.10), channel_id=1, source_target_pairs={{0,1},{1,2},{2,3},{3,4},{4,5},{5,6},{6,7},{8,9},{9,10},{10,11},{11... | collective-permute-start | bytes 3538952 | tf_op jit(solution)/shard_map/ppermute | solution.py:15
  112.5 7.5 %collective-permute-start.4 = (f32[1,2,192,128]{3,2,1,0:T(8,128)}, f32[1,2,192,128]{3,2,1,0:T(8,128)}, u32[]{:S(2)}, u32[]{:S(2)}) collective-permute-start(f32[1,2,192,128]{3,2,1,0:T(8,128)} %get-tuple-element.23), channel_id=1, source_target_pairs={{0,8},{8,16},{16,24},{24,32},{32,40},{40,48},{48,56},{56,64},{64,7... | collective-permute-start | bytes 589832 | tf_op jit(solution)/shard_map/ppermute | solution.py:15
  116.0 7.8 %collective-permute-start.5 = (f32[1,2,192,128]{3,2,1,0:T(8,128)}, f32[1,2,192,128]{3,2,1,0:T(8,128)}, u32[]{:S(2)}, u32[]{:S(2)}) collective-permute-start(f32[1,2,192,128]{3,2,1,0:T(8,128)} %get-tuple-element.24), channel_id=1, source_target_pairs={{8,0},{16,8},{24,16},{32,24},{40,32},{48,40},{56,48},{64,56},{72,6... | collective-permute-start | bytes 589832 | tf_op jit(solution)/shard_map/ppermute | solution.py:18
  125.7 13.2 %collective-permute-start.6 = (f32[4,1,192,128]{3,2,1,0:T(8,128)}, f32[4,1,192,128]{3,2,1,0:T(8,128)}, u32[]{:S(2)}, u32[]{:S(2)}) collective-permute-start(f32[4,1,192,128]{3,2,1,0:T(8,128)} %get-tuple-element.15), channel_id=1, source_target_pairs={{0,1},{1,2},{2,3},{3,4},{4,5},{5,6},{6,7},{8,9},{9,10},{10,11},{11... | collective-permute-start | bytes 1179656 | tf_op jit(solution)/shard_map/ppermute | solution.py:15
  129.3 9.6 %collective-permute-start.7 = (f32[4,1,192,128]{3,2,1,0:T(8,128)}, f32[4,1,192,128]{3,2,1,0:T(8,128)}, u32[]{:S(2)}, u32[]{:S(2)}) collective-permute-start(f32[4,1,192,128]{3,2,1,0:T(8,128)} %get-tuple-element.16), channel_id=1, source_target_pairs={{1,0},{2,1},{3,2},{4,3},{5,4},{6,5},{7,6},{9,8},{10,9},{11,10},{12... | collective-permute-start | bytes 1179656 | tf_op jit(solution)/shard_map/ppermute | solution.py:18
  138.9 10.1 %copy-start = (bf16[4,4,4,192,192]{4,3,2,1,0:T(8,128)(2,1)}, bf16[4,4,4,192,192]{4,3,2,1,0:T(8,128)(2,1)S(1)}, u32[]{:S(2)}) copy-start(bf16[4,4,4,192,192]{4,3,2,1,0:T(8,128)(2,1)S(1)} %pad_maximum_fusion) | copy-start | bytes 14155780
  159.3 4.4 collective-permute-start.9
  161.2 6.8 %collective-permute-start.8 = (bf16[1,2,192,128]{3,2,1,0:T(8,128)(2,1)S(1)}, bf16[1,2,192,128]{3,2,1,0:T(8,128)(2,1)S(1)}, u32[]{:S(2)}, u32[]{:S(2)}) collective-permute-start(bf16[1,2,192,128]{3,2,1,0:T(8,128)(2,1)S(1)} %get-tuple-element.28), channel_id=1, source_target_pairs={{8,0},{16,8},{24,16},{32,24},{40,32},{48,40},{56,48},{64,56},{72,6... | collective-permute-start | bytes 294920 | tf_op jit(solution)/shard_map/ppermute | solution.py:18
  162.5 12.0 %copy-start.7 = (bf16[2,2,192,192]{2,3,1,0:T(8,128)(2,1)S(1)}, bf16[2,2,192,192]{2,3,1,0:T(8,128)(2,1)}, u32[]{:S(2)}) copy-start(bf16[2,2,192,192]{2,3,1,0:T(8,128)(2,1)} %fusion.29) | copy-start | bytes 884740
  163.6 13.5 %copy-start.5 = (bf16[2,2,192,192]{3,2,1,0:T(8,128)(2,1)}, bf16[2,2,192,192]{3,2,1,0:T(8,128)(2,1)S(1)}, u32[]{:S(2)}) copy-start(bf16[2,2,192,192]{3,2,1,0:T(8,128)(2,1)S(1)} %fusion.28) | copy-start | bytes 884740
  163.6 12.3 %copy-start.1 = (bf16[4,2,2,192,192]{4,3,2,1,0:T(8,128)(2,1)S(1)}, bf16[4,2,2,192,192]{4,3,2,1,0:T(8,128)(2,1)}, u32[]{:S(2)}) copy-start(bf16[4,2,2,192,192]{4,3,2,1,0:T(8,128)(2,1)} %param.3) | copy-start | bytes 3538948
  168.2 7.8 %collective-permute-start.10 = (bf16[4,1,192,128]{3,2,1,0:T(8,128)(2,1)S(1)}, bf16[4,1,192,128]{3,2,1,0:T(8,128)(2,1)S(1)}, u32[]{:S(2)}, u32[]{:S(2)}) collective-permute-start(bf16[4,1,192,128]{3,2,1,0:T(8,128)(2,1)S(1)} %get-tuple-element.21), channel_id=1, source_target_pairs={{1,0},{2,1},{3,2},{4,3},{5,4},{6,5},{7,6},{9,8},{10,9},{11,10},{12... | collective-permute-start | bytes 589832 | tf_op jit(solution)/shard_map/ppermute | solution.py:18
  170.1 7.0 %collective-permute-start.11 = (bf16[4,1,192,128]{3,2,1,0:T(8,128)(2,1)S(1)}, bf16[4,1,192,128]{3,2,1,0:T(8,128)(2,1)S(1)}, u32[]{:S(2)}, u32[]{:S(2)}) collective-permute-start(bf16[4,1,192,128]{3,2,1,0:T(8,128)(2,1)S(1)} %get-tuple-element.22), channel_id=1, source_target_pairs={{0,1},{1,2},{2,3},{3,4},{4,5},{5,6},{6,7},{8,9},{9,10},{10,11},{11... | collective-permute-start | bytes 589832 | tf_op jit(solution)/shard_map/ppermute | solution.py:15
  177.4 82.5 %copy-start.4 = (f32[2,2,192,128]{3,2,1,0:T(8,128)S(1)}, f32[2,2,192,128]{3,2,1,0:T(8,128)}, u32[]{:S(2)}) copy-start(f32[2,2,192,128]{3,2,1,0:T(8,128)} %param.2) | copy-start | bytes 1179652
  332.9 6.4 %collective-permute-start.12 = (f32[1,2,192,128]{3,2,1,0:T(8,128)S(1)}, f32[1,2,192,128]{3,2,1,0:T(8,128)S(1)}, u32[]{:S(2)}, u32[]{:S(2)}) collective-permute-start(f32[1,2,192,128]{3,2,1,0:T(8,128)S(1)} %get-tuple-element.19), channel_id=1, source_target_pairs={{0,8},{8,16},{16,24},{24,32},{32,40},{40,48},{48,56},{56,64},{64,7... | collective-permute-start | bytes 589832 | tf_op jit(solution)/shard_map/ppermute | solution.py:15
  335.7 7.3 %collective-permute-start.13 = (f32[1,2,192,128]{3,2,1,0:T(8,128)S(1)}, f32[1,2,192,128]{3,2,1,0:T(8,128)S(1)}, u32[]{:S(2)}, u32[]{:S(2)}) collective-permute-start(f32[1,2,192,128]{3,2,1,0:T(8,128)S(1)} %get-tuple-element.20), channel_id=1, source_target_pairs={{8,0},{16,8},{24,16},{32,24},{40,32},{48,40},{56,48},{64,56},{72,6... | collective-permute-start | bytes 589832 | tf_op jit(solution)/shard_map/ppermute | solution.py:18
  343.0 12.7 %copy-start.9 = (f32[1,2,192,128]{3,2,1,0:T(8,128)}, f32[1,2,192,128]{3,2,1,0:T(8,128)S(1)}, u32[]{:S(2)}) copy-start(f32[1,2,192,128]{3,2,1,0:T(8,128)S(1)} %collective-permute-done.13) | copy-start | bytes 589828
  343.0 16.1 %slice-start = ((s8[6291456]{0:T(1024)(128)(4,1)}), s8[4194304]{0:T(1024)(128)(4,1)S(1)}, s32[]{:S(2)}) async-start(s8[6291456]{0:T(1024)(128)(4,1)} %bitcast.99), calls=%async_computation | async-start | bytes 8388608
  343.1 8.1 %collective-permute-start.14 = (f32[4,1,192,128]{3,2,1,0:T(8,128)S(1)}, f32[4,1,192,128]{3,2,1,0:T(8,128)S(1)}, u32[]{:S(2)}, u32[]{:S(2)}) collective-permute-start(f32[4,1,192,128]{3,2,1,0:T(8,128)S(1)} %get-tuple-element.13), channel_id=1, source_target_pairs={{0,1},{1,2},{2,3},{3,4},{4,5},{5,6},{6,7},{8,9},{9,10},{10,11},{11... | collective-permute-start | bytes 1179656 | tf_op jit(solution)/shard_map/ppermute | solution.py:15
  346.5 12.6 %slice-start.1 = ((s8[6291456]{0:T(1024)(128)(4,1)}), s8[2097152]{0:T(1024)(128)(4,1)S(1)}, s32[]{:S(2)}) async-start(s8[6291456]{0:T(1024)(128)(4,1)} %bitcast.99), calls=%async_computation.1 | async-start | bytes 4194304
  346.5 9.2 %collective-permute-start.15 = (f32[4,1,192,128]{3,2,1,0:T(8,128)S(1)}, f32[4,1,192,128]{3,2,1,0:T(8,128)S(1)}, u32[]{:S(2)}, u32[]{:S(2)}) collective-permute-start(f32[4,1,192,128]{3,2,1,0:T(8,128)S(1)} %get-tuple-element.14), channel_id=1, source_target_pairs={{1,0},{2,1},{3,2},{4,3},{5,4},{6,5},{7,6},{9,8},{10,9},{11,10},{12... | collective-permute-start | bytes 1179656 | tf_op jit(solution)/shard_map/ppermute | solution.py:18
  351.2 7.8 %copy-start.10 = (f32[4,1,192,128]{3,2,1,0:T(8,128)}, f32[4,1,192,128]{3,2,1,0:T(8,128)S(1)}, u32[]{:S(2)}) copy-start(f32[4,1,192,128]{3,2,1,0:T(8,128)S(1)} %collective-permute-done.14) | copy-start | bytes 1179652
  355.8 3.3 copy-start.11
  373.1 16.0 %copy-start.8 = (bf16[2,2,192,192]{2,3,1,0:T(8,128)(2,1)S(1)}, bf16[2,2,192,192]{2,3,1,0:T(8,128)(2,1)}, u32[]{:S(2)}) copy-start(bf16[2,2,192,192]{2,3,1,0:T(8,128)(2,1)} %fusion.29) | copy-start | bytes 884740
  373.1 5.1 collective-permute-start.17
  376.6 6.7 %collective-permute-start.16 = (bf16[1,2,192,128]{3,2,1,0:T(8,128)(2,1)S(1)}, bf16[1,2,192,128]{3,2,1,0:T(8,128)(2,1)S(1)}, u32[]{:S(2)}, u32[]{:S(2)}) collective-permute-start(bf16[1,2,192,128]{3,2,1,0:T(8,128)(2,1)S(1)} %get-tuple-element.26), channel_id=1, source_target_pairs={{8,0},{16,8},{24,16},{32,24},{40,32},{48,40},{56,48},{64,56},{72,6... | collective-permute-start | bytes 294920 | tf_op jit(solution)/shard_map/ppermute | solution.py:18
  383.3 8.4 %copy-start.6 = (bf16[2,2,192,192]{3,2,1,0:T(8,128)(2,1)S(1)}, bf16[2,2,192,192]{3,2,1,0:T(8,128)(2,1)}, u32[]{:S(2)}) copy-start(bf16[2,2,192,192]{3,2,1,0:T(8,128)(2,1)} %copy-done.5) | copy-start | bytes 884740
  383.4 7.1 %collective-permute-start.18 = (bf16[4,1,192,128]{3,2,1,0:T(8,128)(2,1)S(1)}, bf16[4,1,192,128]{3,2,1,0:T(8,128)(2,1)S(1)}, u32[]{:S(2)}, u32[]{:S(2)}) collective-permute-start(bf16[4,1,192,128]{3,2,1,0:T(8,128)(2,1)S(1)} %get-tuple-element.17), channel_id=1, source_target_pairs={{1,0},{2,1},{3,2},{4,3},{5,4},{6,5},{7,6},{9,8},{10,9},{11,10},{12... | collective-permute-start | bytes 589832 | tf_op jit(solution)/shard_map/ppermute | solution.py:18
  385.4 6.2 %collective-permute-start.19 = (bf16[4,1,192,128]{3,2,1,0:T(8,128)(2,1)S(1)}, bf16[4,1,192,128]{3,2,1,0:T(8,128)(2,1)S(1)}, u32[]{:S(2)}, u32[]{:S(2)}) collective-permute-start(bf16[4,1,192,128]{3,2,1,0:T(8,128)(2,1)S(1)} %get-tuple-element.18), channel_id=1, source_target_pairs={{0,1},{1,2},{2,3},{3,4},{4,5},{5,6},{6,7},{8,9},{9,10},{10,11},{11... | collective-permute-start | bytes 589832 | tf_op jit(solution)/shard_map/ppermute | solution.py:15
where the time goes:
time: 550 us; the launch traced here: 549 us
  blocking collectives  401 us (73%)
  starting transfers between devices  51.9 us (9%)
  matrix products  36.8 us (7%)
  waiting for transfers between devices  30.4 us (6%)
  local copies, waits for them, and re-layouts  16.3 us (3%)
  other arithmetic  12.3 us (2%)
    psum x2, blocking collectives, local(): heights = lax.psum(partial_value, ('gx', 'gy'))  163 us
    psum x2, blocking collectives, local(): lax.psum(jnp.sum(projected * projected, axis=(0, 1, 2)), ('gx', 'gy'))  146 us
    psum x1, blocking collectives, local(): lax.psum(jnp.sum(load_vector * load_vector, axis=(0, 1, 2)), ('gx', 'gy'))  91.5 us
    ppermute x10, starting transfers between devices, extended(): lax.ppermute(lax.slice_in_dim(block, block.shape[dim] - width, None, axis...  34.5 us
    dot_general x14, matrix products, local_product(): jnp.einsum('xyij,xyjr->xyir', matrices, operand, preferred_element_type=j...  29 us
    ppermute x10, waiting for transfers between devices, extended(): lax.ppermute(lax.slice_in_dim(block, 0, width, axis=dim), axis, backward)  23.8 us
    ppermute x10, starting transfers between devices, extended(): lax.ppermute(lax.slice_in_dim(block, 0, width, axis=dim), axis, backward)  17.4 us
  transfers between devices with their start and end apart: 20, of which 13 were waited for; matrix products, arithmetic and copies ran while one was open for 3% of the time, Pallas kernels for 0%

commit v1 on v0

v1 whole, which is shorter than its diff:
```python
import functools

import jax
import jax.numpy as jnp
from jax import lax
from jax.experimental import pallas as pl
from jax.experimental.pallas import tpu as pltpu
from jax.sharding import PartitionSpec as P

MESH = pl.DeviceIdType.MESH
F32 = jnp.float32
BF16 = jnp.bfloat16
NODES = [(0, 0), (0, 1), (1, 0), (1, 1)]
XL, XH, YL, YH = range(4)
SUMS = 3
TERMS = 4


def dot(a, b):
    return jnp.dot(a, b, preferred_element_type=F32)


def split(u):
    high = u.astype(BF16)
    return high, (u - high.astype(F32)).astype(BF16)


def dot2(a, u):
    high, low = split(u)
    return dot(a, high) + dot(a, low)


def over_rows(a):
    return jnp.sum(a, axis=0, keepdims=True)


def kernel(
    ngx, ngy, fast,
    load_ref, blocks_ref, out_ref,
    v, m, t1, t2, sent, products, halo, first, total, c1, c2, w, q,
    mine, landed,
    load_sem, halo_send, halo_recv, sum_send, sum_recv,
):
    gx, gy = lax.axis_index("gx"), lax.axis_index("gy")
    up_x, down_x = lax.rem(gx + 1, ngx), lax.rem(gx + ngx - 1, ngx)
    up_y, down_y = lax.rem(gy + 1, ngy), lax.rem(gy + ngy - 1, ngy)
    sides = {XL: (up_x, gy), XH: (down_x, gy), YL: (gx, up_y), YH: (gx, down_y)}

    slow = ngx // fast
    chips = ngy // 2
    along, across = gx // fast, gx % fast
    chip, core = gy // 2, gy % 2
    groups = [
        [
            (lax.rem(along + d, slow) * fast + across, chip * 2 + lax.rem(core + e, 2))
            for d in range(slow)
            for e in range(2)
            if d or e
        ],
        [
            (along * fast + lax.rem(across + d, fast), lax.rem(chip + e, chips) * 2 + core)
            for d in range(fast)
            for e in range(chips)
            if d or e
        ],
    ]

    loads = [
        pltpu.make_async_copy(load_ref, v, load_sem.at[0]),
        pltpu.make_async_copy(blocks_ref.at[3], m.at[3], load_sem.at[1]),
        pltpu.make_async_copy(blocks_ref.at[1], m.at[1], load_sem.at[2]),
        pltpu.make_async_copy(blocks_ref.at[2], m.at[2], load_sem.at[3]),
        pltpu.make_async_copy(blocks_ref.at[0], m.at[0], load_sem.at[4]),
    ]
    for copy in loads:
        copy.start()

    barrier = pltpu.get_barrier_semaphore()
    partners = [*sides.values(), *groups[0], *groups[1]]
    for partner in partners:
        pl.semaphore_signal(barrier, inc=1, device_id=partner, device_id_type=MESH)

    started = []

    def send(source, step, side, place):
        slot = side * 2 + place
        copy = pltpu.make_async_remote_copy(
            src_ref=source,
            dst_ref=halo.at[step, side, place],
            send_sem=halo_send.at[step, slot],
            recv_sem=halo_recv.at[step, slot],
            device_id=sides[side],
            device_id_type=MESH,
        )
        copy.start()
        started.append(copy)
        arriving[step, side, place] = copy

    arriving = {}
    spreading = {}

    def exchange(step, field):
        for i, j in NODES:
            sent[step, i, j] = field[i, j].astype(BF16)
            if i == 0:
                send(sent.at[step, i, j], step, XH, j)
        for j in range(2):
            products[step, 0, j] = dot2(t1[1, j], field[1, j]).astype(BF16)
            send(products.at[step, 0, j], step, XL, j)
        for i in range(2):
            send(sent.at[step, i, 0], step, YH, i)
        for i in range(2):
            products[step, 1, i] = dot2(t2[i, 1], field[i, 1]).astype(BF16)
            send(products.at[step, 1, i], step, YL, i)

    def inner(step, field):
        for i, j in NODES:
            value = dot2(m[0, i, j], field[i, j])
            value += dot(m[1, 0, j], sent[step, 1, j]) if i == 0 else dot(t1[0, j], sent[step, 0, j])
            value += dot(m[2, i, 0], sent[step, i, 1]) if j == 0 else dot(t2[i, 0], sent[step, i, 0])
            total[i, j] = value

    def outer(step, i, j):
        value = total[i, j]
        if j == 0:
            arriving[step, YL, i].wait_recv()
            value += halo[step, YL, i].astype(F32)
        else:
            arriving[step, YH, i].wait_recv()
            value += dot(m[2, i, 1], halo[step, YH, i])
        if i == 0:
            arriving[step, XL, j].wait_recv()
            value += halo[step, XL, j].astype(F32)
        else:
            arriving[step, XH, j].wait_recv()
            value += dot(m[1, 1, j], halo[step, XH, j])
        return value

    def spread(number, phase, rows):
        for term, row in enumerate(rows):
            mine[number, phase, pl.ds(term, 1)] = row
        copies = []
        for slot, partner in enumerate(groups[phase]):
            copy = pltpu.make_async_remote_copy(
                src_ref=mine.at[number, phase],
                dst_ref=landed.at[number, phase, slot],
                send_sem=sum_send.at[number, phase, slot],
                recv_sem=sum_recv.at[number, phase, slot],
                device_id=partner,
                device_id_type=MESH,
            )
            copy.start()
            copies.append(copy)
        started.extend(copies)
        spreading[number, phase] = copies

    def gather(number, phase, count):
        value = mine[number, phase]
        for slot, copy in enumerate(spreading[number, phase]):
            copy.wait_recv()
            value += landed[number, phase, slot]
        return [value[term : term + 1] for term in range(count)]

    def inner_products(*pairs):
        rows = []
        for a, b in pairs:
            row = None
            for i, j in NODES:
                part = over_rows(a[i, j] * b[i, j])
                row = part if row is None else row + part
            rows.append(row)
        return rows

    for number in range(SUMS):
        for phase in range(2):
            mine[number, phase] = jnp.zeros_like(mine[number, phase])

    loads[2].wait()
    loads[3].wait()

    @pl.when(gx == ngx - 1)
    def _():
        for j in range(2):
            m[1, 1, j] = jnp.zeros_like(m[1, 1, j])

    @pl.when(gy == ngy - 1)
    def _():
        for i in range(2):
            m[2, i, 1] = jnp.zeros_like(m[2, i, 1])

    for i, j in NODES:
        t1[i, j] = m[1, i, j].T
        t2[i, j] = m[2, i, j].T

    loads[0].wait()
    loads[1].wait()
    for i, j in NODES:
        first[i, j] = dot2(m[3, i, j], v[i, j])
    pl.semaphore_wait(barrier, len(partners))
    exchange(0, first)
    spread(0, 0, inner_products((v, v)))
    loads[4].wait()
    inner(0, first)
    for i, j in NODES:
        c1[i, j] = first[i, j] + dot2(m[3, i, j], v[i, j] - outer(0, i, j))
    exchange(1, c1)
    spread(0, 1, gather(0, 0, 1))
    inner(1, c1)
    (square,) = gather(0, 1, 1)
    norm = jnp.sqrt(square)
    for i, j in NODES:
        w[i, j] = outer(1, i, j) / norm
        first[i, j] = dot2(m[3, i, j], w[i, j])
    exchange(2, first)
    for i, j in NODES:
        v[i, j] = v[i, j] / norm
    spread(1, 0, inner_products((w, w), (w, v)))
    inner(2, first)
    for i, j in NODES:
        c2[i, j] = first[i, j] + dot2(m[3, i, j], w[i, j] - outer(2, i, j))
    exchange(3, c2)
    spread(1, 1, gather(1, 0, 2))
    inner(3, c2)
    ww, wb = gather(1, 1, 2)
    size = jnp.sqrt(ww)
    scale = 1.0 / size
    for i, j in NODES:
        q[i, j] = outer(3, i, j) * scale
    spread(2, 0, inner_products((w, q), (q, q), (v, q)))
    spread(2, 1, gather(2, 0, 3))
    wq, qq, bq = gather(2, 1, 3)
    wq = wq * scale
    wb = wb * scale
    second = (bq - wq * wb) / (qq - wq * wq)
    weight_1 = (wb - wq * second) * scale
    weight_2 = second * scale * norm
    for i, j in NODES:
        out_ref[i, j] = weight_1 * c1[i, j] + weight_2 * c2[i, j]
    for copy in started:
        copy.wait_send()


def solution(mesh):
    ngx, ngy = mesh.shape["gx"], mesh.shape["gy"]
    fast = 4

    def local(load_vector, blocks):
        cx, cy, size, cases = load_vector.shape
        field = (cx, cy, size, cases)
        matrices = (cx, cy, size, size)
        sem = pltpu.SemaphoreType.DMA
        return pl.pallas_call(
            functools.partial(kernel, ngx, ngy, fast),
            out_shape=jax.ShapeDtypeStruct(field, F32),
            in_specs=[pl.BlockSpec(memory_space=pl.ANY)] * 2,
            out_specs=pl.BlockSpec(memory_space=pltpu.VMEM),
            scratch_shapes=[
                pltpu.VMEM(field, F32),
                pltpu.VMEM((4, *matrices), BF16),
                pltpu.VMEM(matrices, BF16),
                pltpu.VMEM(matrices, BF16),
                pltpu.VMEM((4, *field), BF16),
                pltpu.VMEM((4, 2, 2, size, cases), BF16),
                pltpu.VMEM((4, 4, 2, size, cases), BF16),
                pltpu.VMEM(field, F32),
                pltpu.VMEM(field, F32),
                pltpu.VMEM(field, F32),
                pltpu.VMEM(field, F32),
                pltpu.VMEM(field, F32),
                pltpu.VMEM(field, F32),
                pltpu.VMEM((SUMS, 2, TERMS, cases), F32),
                pltpu.VMEM((SUMS, 2, 15, TERMS, cases), F32),
                sem((5,)),
                sem((4, 8)),
                sem((4, 8)),
                sem((SUMS, 2, 15)),
                sem((SUMS, 2, 15)),
            ],
            compiler_params=pltpu.CompilerParams(
                collective_id=0, has_side_effects=True, vmem_limit_bytes=48 * 1024 * 1024
            ),
        )(load_vector, blocks)

    return jax.shard_map(
        local,
        mesh=mesh,
        in_specs=(P("gx", "gy", None, None), P(None, "gx", "gy", None, None)),
        out_specs=P("gx", "gy", None, None),
        check_vma=False,
    )
```

time: 550 us -> 53.6 us (0.10)
  blocking collectives: 401 us -> 0 us
  starting transfers between devices: 51.9 us -> 0 us
  Pallas kernels: 0 us -> 50.3 us
  matrix products: 36.8 us -> 0 us
  waiting for transfers between devices: 30.4 us -> 0 us
  local copies, waits for them, and re-layouts: 16.3 us -> 3.15 us
  other arithmetic: 12.3 us -> 0 us
    psum x5 -> x0, blocking collectives: 401 us -> none  [the longest x2 163 us: local(): heights = lax.psum(partial_value, ('gx', 'gy'))]
    ppermute x20 -> x0, starting transfers between devices: 51.9 us -> none  [the longest x10 34.5 us: extended(): lax.ppermute(lax.slice_in_dim(block, block.shape[dim] - width, None, axis...]
    pallas_call x0 -> x1, Pallas kernels: none -> 50.3 us  [local(): pl.pallas_call(functools.partial(kernel, ngx, ngy, fast), out_shape=jax.S...]
    ppermute x20 -> x0, waiting for transfers between devices: 30.4 us -> none  [the longest x10 23.8 us: extended(): lax.ppermute(lax.slice_in_dim(block, 0, width, axis=dim), axis, backward)]
    dot_general x18 -> x0, matrix products: 30.2 us -> none  [the longest x14 29 us: local_product(): jnp.einsum('xyij,xyjr->xyir', matrices, operand, preferred_element_type=j...]
    slice x14 -> x0, local copies, waits for them, and re-layouts: 7.14 us -> none  [the longest x4 4.34 us: extended(): lax.slice_in_dim(block, 0, width, axis=dim)]
    slice x4 -> x0, matrix products: 6.63 us -> none  [the longest x2 3.33 us: couple_box(): local_transposed(blocks[1], operand)[:-1]]
  transfers between devices with their start and end apart: 20 -> 0, of which waited for: 13 -> 0; matrix products, arithmetic and copies ran while one was open for 3% -> 0% of each run, Pallas kernels for 0% -> 0%
where the time goes in v1:
time: 53.6 us; the launch traced here: 53.5 us
  Pallas kernels  50.3 us (94%)
  local copies, waits for them, and re-layouts  3.15 us (6%)
    pallas_call x1, Pallas kernels, local(): pl.pallas_call(functools.partial(kernel, ngx, ngy, fast), out_shape=jax.S...  50.3 us
    unnamed x5, local copies, waits for them, and re-layouts  3.15 us

profile of v1, /device:TPU:1, one launch (start us, length us, event | category | flops | bytes accessed | tf_op | source)
XLA Modules:
  0.0 53.5 jit_solution(17150786403532669969)
XLA Ops:
  0.0 0.0 copy-start
  0.0 1.4 %copy-done = bf16[4,2,2,192,192]{4,3,2,1,0:T(8,128)(2,1)S(1)} copy-done((bf16[4,2,2,192,192]{4,3,2,1,0:T(8,128)(2,1)S(1)}, bf16[4,2,2,192,192]{4,3,2,1,0:T(8,128)(2,1)}, u32[]{:S(2)}) %copy-start) | copy-done | bytes 1179672
  1.4 0.0 copy-start.1
  1.4 1.0 %copy-done.1 = f32[2,2,192,128]{3,2,1,0:T(8,128)S(1)} copy-done((f32[2,2,192,128]{3,2,1,0:T(8,128)S(1)}, f32[2,2,192,128]{3,2,1,0:T(8,128)}, u32[]{:S(2)}) %copy-start.1) | copy-done | bytes 393240
  2.4 50.3 %shard_map.28 = f32[2,2,192,128]{3,2,1,0:T(8,128)S(1)} custom-call(f32[2,2,192,128]{3,2,1,0:T(8,128)S(1)} %copy-done.1, bf16[4,2,2,192,192]{4,3,2,1,0:T(8,128)(2,1)S(1)} %copy-done), custom_call_target="tpu_custom_call" | custom-call | tf_op jit(solution)/shard_map/pallas_call | solution.py:252
  52.7 0.7 %copy.4 = f32[2,2,192,128]{3,2,1,0:T(8,128)} copy(f32[2,2,192,128]{3,2,1,0:T(8,128)S(1)} %shard_map.28) | data formatting | bytes 786432
Async XLA Ops:
  0.0 1.4 %copy-start = (bf16[4,2,2,192,192]{4,3,2,1,0:T(8,128)(2,1)S(1)}, bf16[4,2,2,192,192]{4,3,2,1,0:T(8,128)(2,1)}, u32[]{:S(2)}) copy-start(bf16[4,2,2,192,192]{4,3,2,1,0:T(8,128)(2,1)} %blocks_ref.1) | copy-start | bytes 3538948
  1.4 1.0 %copy-start.1 = (f32[2,2,192,128]{3,2,1,0:T(8,128)S(1)}, f32[2,2,192,128]{3,2,1,0:T(8,128)}, u32[]{:S(2)}) copy-start(f32[2,2,192,128]{3,2,1,0:T(8,128)} %load_ref.1) | copy-start | bytes 1179652

commit v2 on v1

v2 whole, which is shorter than its diff:
```python
import functools

import jax
import jax.numpy as jnp
from jax import lax
from jax.experimental import pallas as pl
from jax.experimental.pallas import tpu as pltpu
from jax.sharding import PartitionSpec as P

MESH = pl.DeviceIdType.MESH
F32 = jnp.float32
BF16 = jnp.bfloat16
NODES = [(0, 0), (1, 0), (0, 1), (1, 1)]
XL, XH, YL, YH = range(4)
TERMS = (1, 2, 4)


def dot(a, b):
    return jnp.dot(a, b, preferred_element_type=F32)


def split(u):
    high = u.astype(BF16)
    return high, (u - high.astype(F32)).astype(BF16)


def dot2(a, u):
    both = dot(a, jnp.concatenate(split(u), axis=1))
    half = u.shape[1]
    return both[:, :half] + both[:, half:]


def over_rows(a):
    return jnp.sum(a, axis=0, keepdims=True)


def kernel(
    ngx, ngy, fast,
    load_ref, blocks_ref, out_ref,
    v, m, t1, t2, sent, products, halo, first, total, c1, c2, w, q,
    mine_0, mine_1, mine_2, landed_0, landed_1, landed_2,
    load_sem, halo_send, halo_recv, sum_send, sum_recv,
):
    gx, gy = lax.axis_index("gx"), lax.axis_index("gy")
    up_x, down_x = lax.rem(gx + 1, ngx), lax.rem(gx + ngx - 1, ngx)
    up_y, down_y = lax.rem(gy + 1, ngy), lax.rem(gy + ngy - 1, ngy)
    sides = {XL: (up_x, gy), XH: (down_x, gy), YL: (gx, up_y), YH: (gx, down_y)}

    slow = ngx // fast
    chips = ngy // 2
    along, across = gx // fast, gx % fast
    chip, core = gy // 2, gy % 2
    groups = [
        [
            (lax.rem(along + d, slow) * fast + across, chip * 2 + lax.rem(core + e, 2))
            for d in range(slow)
            for e in range(2)
            if d or e
        ],
        [
            (along * fast + lax.rem(across + d, fast), lax.rem(chip + e, chips) * 2 + core)
            for d in range(fast)
            for e in range(chips)
            if d or e
        ],
    ]
    mine = [mine_0, mine_1, mine_2]
    landed = [landed_0, landed_1, landed_2]

    barrier = pltpu.get_barrier_semaphore()
    partners = [*groups[0], *groups[1], *sides.values()]
    for partner in partners:
        pl.semaphore_signal(barrier, inc=1, device_id=partner, device_id_type=MESH)

    loads = [
        pltpu.make_async_copy(load_ref, v, load_sem.at[0]),
        pltpu.make_async_copy(blocks_ref.at[3], m.at[3], load_sem.at[1]),
        pltpu.make_async_copy(blocks_ref.at[1], m.at[1], load_sem.at[2]),
        pltpu.make_async_copy(blocks_ref.at[2], m.at[2], load_sem.at[3]),
        pltpu.make_async_copy(blocks_ref.at[0], m.at[0], load_sem.at[4]),
    ]
    for copy in loads:
        copy.start()

    arriving = {}

    def send(source, step, side, place):
        slot = side * 2 + place
        copy = pltpu.make_async_remote_copy(
            src_ref=source,
            dst_ref=halo.at[step, side, place],
            send_sem=halo_send.at[step, slot],
            recv_sem=halo_recv.at[step, slot],
            device_id=sides[side],
            device_id_type=MESH,
        )
        copy.start()
        arriving[step, side, place] = copy

    def announce(step, i, j):
        if i == 0:
            send(sent.at[step, i, j], step, XH, j)
        if j == 0:
            send(sent.at[step, i, j], step, YH, i)

    def pass_up(step, i, j):
        if i == 1:
            products[step, 0, j] = dot(t1[1, j], sent[step, 1, j]).astype(BF16)
            send(products.at[step, 0, j], step, XL, j)
        if j == 1:
            products[step, 1, i] = dot(t2[i, 1], sent[step, i, 1]).astype(BF16)
            send(products.at[step, 1, i], step, YL, i)

    def exchange(step, field, compute):
        for i, j in NODES:
            value = compute(i, j)
            field[i, j] = value
            sent[step, i, j] = value.astype(BF16)
            announce(step, i, j)
            pass_up(step, i, j)

    def inner(step, field):
        for i, j in NODES:
            value = dot2(m[0, i, j], field[i, j]) if step < 3 else dot(m[0, i, j], sent[step, i, j])
            value += dot(m[1, 0, j], sent[step, 1, j]) if i == 0 else dot(t1[0, j], sent[step, 0, j])
            value += dot(m[2, i, 0], sent[step, i, 1]) if j == 0 else dot(t2[i, 0], sent[step, i, 0])
            total[i, j] = value

    def outer(step, i, j):
        value = total[i, j]
        if j == 0:
            arriving[step, YL, i].wait_recv()
            value += halo[step, YL, i].astype(F32)
        else:
            arriving[step, YH, i].wait_recv()
            value += dot(m[2, i, 1], halo[step, YH, i])
        if i == 0:
            arriving[step, XL, j].wait_recv()
            value += halo[step, XL, j].astype(F32)
        else:
            arriving[step, XH, j].wait_recv()
            value += dot(m[1, 1, j], halo[step, XH, j])
        return value

    def spread(number, phase, rows):
        for term, row in enumerate(rows):
            mine[number][phase, pl.ds(term, 1)] = row
        for slot, partner in enumerate(groups[phase]):
            pltpu.make_async_remote_copy(
                src_ref=mine[number].at[phase],
                dst_ref=landed[number].at[phase, slot],
                send_sem=sum_send.at[number, phase],
                recv_sem=sum_recv.at[number, phase],
                device_id=partner,
                device_id_type=MESH,
            ).start()

    def all_landed(number, phase):
        return pltpu.make_async_remote_copy(
            src_ref=landed[number].at[phase],
            dst_ref=landed[number].at[phase],
            send_sem=sum_send.at[number, phase],
            recv_sem=sum_recv.at[number, phase],
            device_id=groups[phase][0],
            device_id_type=MESH,
        )

    def gather(number, phase, count):
        all_landed(number, phase).wait_recv()
        value = mine[number][phase]
        for slot in range(len(groups[phase])):
            value += landed[number][phase, slot]
        return [value[term : term + 1] for term in range(count)]

    def inner_products(*pairs):
        rows = [None] * len(pairs)
        for i, j in NODES:
            for term, (a, b) in enumerate(pairs):
                part = over_rows(a(i, j) * b(i, j))
                rows[term] = part if rows[term] is None else rows[term] + part
        return rows

    mine_2[...] = jnp.zeros(mine_2.shape, F32)

    loads[0].wait()
    loads[1].wait()
    for i, j in NODES:
        value = dot2(m[3, i, j], v[i, j])
        first[i, j] = value
        sent[0, i, j] = value.astype(BF16)
    pl.semaphore_wait(barrier, len(partners))
    for i, j in NODES:
        announce(0, i, j)
    loads[2].wait()
    loads[3].wait()

    @pl.when(gx == ngx - 1)
    def _():
        for j in range(2):
            m[1, 1, j] = jnp.zeros_like(m[1, 1, j])

    @pl.when(gy == ngy - 1)
    def _():
        for i in range(2):
            m[2, i, 1] = jnp.zeros_like(m[2, i, 1])

    for k in range(2):
        t1[1, k] = m[1, 1, k].T
    for k in range(2):
        t2[k, 1] = m[2, k, 1].T
    for i, j in NODES:
        pass_up(0, i, j)
    spread(0, 0, inner_products((lambda i, j: v[i, j], lambda i, j: v[i, j])))
    for k in range(2):
        t1[0, k] = m[1, 0, k].T
        t2[k, 0] = m[2, k, 0].T
    loads[4].wait()
    inner(0, first)

    exchange(1, c1, lambda i, j: first[i, j] + dot2(m[3, i, j], v[i, j] - outer(0, i, j)))
    inner(1, c1)
    spread(0, 1, gather(0, 0, 1))

    def second_start(i, j):
        w[i, j] = outer(1, i, j)
        return dot2(m[3, i, j], w[i, j])

    exchange(2, first, second_start)
    (square,) = gather(0, 1, 1)
    norm = jnp.sqrt(square)
    inverse = 1.0 / norm
    scaled_w = lambda i, j: w[i, j] * inverse
    scaled_v = lambda i, j: v[i, j] * inverse
    spread(1, 0, inner_products((scaled_w, scaled_w), (scaled_w, scaled_v)))
    inner(2, first)

    exchange(3, c2, lambda i, j: first[i, j] + dot2(m[3, i, j], w[i, j] - outer(2, i, j)))
    inner(3, c2)
    spread(1, 1, gather(1, 0, 2))
    for i, j in NODES:
        q[i, j] = outer(3, i, j)
    ww, wb = gather(1, 1, 2)
    scale = 1.0 / jnp.sqrt(ww)
    both = inverse * scale
    unit_w = lambda i, j: w[i, j] * both
    unit_q = lambda i, j: q[i, j] * both
    spread(2, 0, inner_products((unit_w, unit_q), (unit_q, unit_q), (scaled_v, unit_q)))
    for copy in arriving.values():
        copy.wait_send()
    for number in range(2):
        for phase in range(2):
            all_landed(number, phase).wait_send()
    spread(2, 1, gather(2, 0, 4)[:3])
    all_landed(2, 0).wait_send()
    wq, qq, bq = gather(2, 1, 3)
    wb = wb * scale
    second = (bq - wq * wb) / (qq - wq * wq)
    weight_1 = (wb - wq * second) * scale
    weight_2 = second * scale
    for i, j in NODES:
        out_ref[i, j] = weight_1 * c1[i, j] + weight_2 * c2[i, j]
    all_landed(2, 1).wait_send()


def solution(mesh):
    ngx, ngy = mesh.shape["gx"], mesh.shape["gy"]
    fast = 4
    others = 2 * (ngx // fast) - 1

    def local(load_vector, blocks):
        cx, cy, size, cases = load_vector.shape
        field = (cx, cy, size, cases)
        matrices = (cx, cy, size, size)
        sem = pltpu.SemaphoreType.DMA
        return pl.pallas_call(
            functools.partial(kernel, ngx, ngy, fast),
            out_shape=jax.ShapeDtypeStruct(field, F32),
            in_specs=[pl.BlockSpec(memory_space=pltpu.HBM)] * 2,
            out_specs=pl.BlockSpec(memory_space=pltpu.VMEM),
            scratch_shapes=[
                pltpu.VMEM(field, F32),
                pltpu.VMEM((4, *matrices), BF16),
                pltpu.VMEM(matrices, BF16),
                pltpu.VMEM(matrices, BF16),
                pltpu.VMEM((4, *field), BF16),
                pltpu.VMEM((4, 2, 2, size, cases), BF16),
                pltpu.VMEM((4, 4, 2, size, cases), BF16),
                pltpu.VMEM(field, F32),
                pltpu.VMEM(field, F32),
                pltpu.VMEM(field, F32),
                pltpu.VMEM(field, F32),
                pltpu.VMEM(field, F32),
                pltpu.VMEM(field, F32),
                *[pltpu.VMEM((2, terms, cases), F32) for terms in TERMS],
                *[pltpu.VMEM((2, others, terms, cases), F32) for terms in TERMS],
                sem((5,)),
                sem((4, 8)),
                sem((4, 8)),
                sem((len(TERMS), 2)),
                sem((len(TERMS), 2)),
            ],
            compiler_params=pltpu.CompilerParams(
                collective_id=0, has_side_effects=True, vmem_limit_bytes=48 * 1024 * 1024
            ),
        )(*[pltpu.with_memory_space_constraint(a, pltpu.HBM) for a in (load_vector, blocks)])

    return jax.shard_map(
        local,
        mesh=mesh,
        in_specs=(P("gx", "gy", None, None), P(None, "gx", "gy", None, None)),
        out_specs=P("gx", "gy", None, None),
        check_vma=False,
    )
```

time: 53.6 us -> 43.9 us (0.82)
  Pallas kernels: 50.3 us -> 43 us
  local copies, waits for them, and re-layouts: 3.15 us -> 0.75 us
    pallas_call x1, Pallas kernels: 50.3 us -> 43 us  [local(): pl.pallas_call(functools.partial(kernel, ngx, ngy, fast), out_shape=jax.S...]
    unnamed x5 -> x1, local copies, waits for them, and re-layouts: 3.15 us -> 0.75 us
where the time goes in v2:
time: 43.9 us; the launch traced here: 43.8 us
  Pallas kernels  43 us (98%)
  local copies, waits for them, and re-layouts  0.75 us (2%)
    pallas_call x1, Pallas kernels, local(): pl.pallas_call(functools.partial(kernel, ngx, ngy, fast), out_shape=jax.S...  43 us

profile of v2, /device:TPU:1, one launch (start us, length us, event | category | flops | bytes accessed | tf_op | source)
XLA Modules:
  0.0 43.8 jit_solution(8777704141789326159)
XLA Ops:
  0.0 43.0 %shard_map.28 = f32[2,2,192,128]{3,2,1,0:T(8,128)S(1)} custom-call(f32[2,2,192,128]{3,2,1,0:T(8,128)} %load_ref.1, bf16[4,2,2,192,192]{4,3,2,1,0:T(8,128)(2,1)} %blocks_ref.1), custom_call_target="tpu_custom_call" | custom-call | tf_op jit(solution)/shard_map/pallas_call | solution.py:275
  43.1 0.7 %copy.4 = f32[2,2,192,128]{3,2,1,0:T(8,128)} copy(f32[2,2,192,128]{3,2,1,0:T(8,128)S(1)} %shard_map.28) | data formatting | bytes 786432

commit v3 on v2

--- a/solution.py
+++ b/solution.py
@@ -12,7 +12,7 @@
 BF16 = jnp.bfloat16
 NODES = [(0, 0), (1, 0), (0, 1), (1, 1)]
 XL, XH, YL, YH = range(4)
-TERMS = (1, 2, 4)
+TERMS = (1, 4, 4)
 
 
 def dot(a, b):
@@ -30,6 +30,14 @@
     return both[:, :half] + both[:, half:]
 
 
+def shrink_of(square):
+    return jnp.where(square > 0.0, jnp.minimum(1.0 / jnp.sqrt(square), 1e12), 1.0)
+
+
+def extra_of(square):
+    return jnp.where(square > 0.0, jnp.minimum(1.0 / jnp.sqrt(square), 1e12), 1e-8)
+
+
 def over_rows(a):
     return jnp.sum(a, axis=0, keepdims=True)
 
@@ -37,38 +45,53 @@
 def kernel(
     ngx, ngy, fast,
     load_ref, blocks_ref, out_ref,
-    v, m, t1, t2, sent, products, halo, first, total, c1, c2, w, q,
+    v, m, t1, t2, sent, products, halo, first, total, c1, c2, w, scaled_w, scaled_v,
     mine_0, mine_1, mine_2, landed_0, landed_1, landed_2,
-    load_sem, halo_send, halo_recv, sum_send, sum_recv,
+    load_sem, halo_send, halo_recv, sum_send, sum_recv, circle,
 ):
     gx, gy = lax.axis_index("gx"), lax.axis_index("gy")
     up_x, down_x = lax.rem(gx + 1, ngx), lax.rem(gx + ngx - 1, ngx)
     up_y, down_y = lax.rem(gy + 1, ngy), lax.rem(gy + ngy - 1, ngy)
     sides = {XL: (up_x, gy), XH: (down_x, gy), YL: (gx, up_y), YH: (gx, down_y)}
 
-    slow = ngx // fast
-    chips = ngy // 2
-    along, across = gx // fast, gx % fast
-    chip, core = gy // 2, gy % 2
+    shape = (ngx // fast, fast, ngy // 2, 2)
+    z, y, x, core = gx // fast, gx % fast, gy // 2, gy % 2
+
+    def device(offset):
+        dz, dy, dx, dc = offset
+        return (
+            lax.rem(z + dz, shape[0]) * fast + lax.rem(y + dy, shape[1]),
+            lax.rem(x + dx, shape[2]) * 2 + lax.rem(core + dc, 2),
+        )
+
+    def offsets(*steps):
+        wrapped = [tuple(d % n for d, n in zip(step, shape)) for step in steps]
+        return [step for step in dict.fromkeys(wrapped) if any(step)]
+
+    def hops(offset):
+        return sum(min(d, n - d) for d, n in zip(offset, shape))
+
+    ranges = [range(n) for n in shape]
     groups = [
-        [
-            (lax.rem(along + d, slow) * fast + across, chip * 2 + lax.rem(core + e, 2))
-            for d in range(slow)
-            for e in range(2)
-            if d or e
-        ],
-        [
-            (along * fast + lax.rem(across + d, fast), lax.rem(chip + e, chips) * 2 + core)
-            for d in range(fast)
-            for e in range(chips)
-            if d or e
-        ],
+        [device(step) for step in sorted(offsets(*steps), key=hops, reverse=True)]
+        for steps in (
+            [(dz, 0, 0, dc) for dz in ranges[0] for dc in ranges[3]],
+            [(0, dy, dx, 0) for dy in ranges[1] for dx in ranges[2]],
+        )
     ]
+    near = [
+        device(step)
+        for step in offsets(
+            (0, 0, 0, 1), (1, 0, 0, 0), (-1, 0, 0, 0), (1, 0, 0, 1), (-1, 0, 0, 1),
+            (0, 1, 0, 0), (0, -1, 0, 0), (0, 0, 1, 0), (0, 0, -1, 0),
+        )
+    ]
+    far = [device(step) for step in offsets((2, 0, 0, 0), (-2, 0, 0, 0), (0, 2, 0, 0), (0, 0, 2, 0))]
     mine = [mine_0, mine_1, mine_2]
     landed = [landed_0, landed_1, landed_2]
 
     barrier = pltpu.get_barrier_semaphore()
-    partners = [*groups[0], *groups[1], *sides.values()]
+    partners = [*sides.values(), *near]
     for partner in partners:
         pl.semaphore_signal(barrier, inc=1, device_id=partner, device_id_type=MESH)
 
@@ -176,10 +199,11 @@
         rows = [None] * len(pairs)
         for i, j in NODES:
             for term, (a, b) in enumerate(pairs):
-                part = over_rows(a(i, j) * b(i, j))
+                part = over_rows(a[i, j] * b[i, j])
                 rows[term] = part if rows[term] is None else rows[term] + part
         return rows
 
+    mine_1[...] = jnp.zeros(mine_1.shape, F32)
     mine_2[...] = jnp.zeros(mine_2.shape, F32)
 
     loads[0].wait()
@@ -191,6 +215,8 @@
     pl.semaphore_wait(barrier, len(partners))
     for i, j in NODES:
         announce(0, i, j)
+    for partner in near:
+        pl.semaphore_signal(circle.at[0], inc=1, device_id=partner, device_id_type=MESH)
     loads[2].wait()
     loads[3].wait()
 
@@ -210,50 +236,74 @@
         t2[k, 1] = m[2, k, 1].T
     for i, j in NODES:
         pass_up(0, i, j)
-    spread(0, 0, inner_products((lambda i, j: v[i, j], lambda i, j: v[i, j])))
     for k in range(2):
         t1[0, k] = m[1, 0, k].T
         t2[k, 0] = m[2, k, 0].T
     loads[4].wait()
     inner(0, first)
+    pl.semaphore_wait(circle.at[0], len(near))
+    for partner in far:
+        pl.semaphore_signal(circle.at[1], inc=1, device_id=partner, device_id_type=MESH)
 
     exchange(1, c1, lambda i, j: first[i, j] + dot2(m[3, i, j], v[i, j] - outer(0, i, j)))
+    pl.semaphore_wait(circle.at[1], len(far))
+    spread(0, 0, inner_products((v, v)))
     inner(1, c1)
-    spread(0, 1, gather(0, 0, 1))
 
     def second_start(i, j):
         w[i, j] = outer(1, i, j)
         return dot2(m[3, i, j], w[i, j])
 
     exchange(2, first, second_start)
-    (square,) = gather(0, 1, 1)
-    norm = jnp.sqrt(square)
-    inverse = 1.0 / norm
-    scaled_w = lambda i, j: w[i, j] * inverse
-    scaled_v = lambda i, j: v[i, j] * inverse
+    (square,) = gather(0, 0, 1)
+    shrink = shrink_of(square)
+    for i, j in NODES:
+        scaled_w[i, j] = w[i, j] * shrink
+        scaled_v[i, j] = v[i, j] * shrink
     spread(1, 0, inner_products((scaled_w, scaled_w), (scaled_w, scaled_v)))
     inner(2, first)
 
     exchange(3, c2, lambda i, j: first[i, j] + dot2(m[3, i, j], w[i, j] - outer(2, i, j)))
     inner(3, c2)
-    spread(1, 1, gather(1, 0, 2))
-    for i, j in NODES:
-        q[i, j] = outer(3, i, j)
-    ww, wb = gather(1, 1, 2)
-    scale = 1.0 / jnp.sqrt(ww)
-    both = inverse * scale
-    unit_w = lambda i, j: w[i, j] * both
-    unit_q = lambda i, j: q[i, j] * both
-    spread(2, 0, inner_products((unit_w, unit_q), (unit_q, unit_q), (scaled_v, unit_q)))
+    ww, wb = gather(1, 0, 2)
+    extra = extra_of(ww)
+    both = shrink * extra
+    rows = [None] * 3
+    for i, j in NODES:
+        unit_q = outer(3, i, j) * both
+        for term, other in enumerate((scaled_w[i, j], unit_q, scaled_v[i, j])):
+            part = over_rows(other * unit_q)
+            rows[term] = part if rows[term] is None else rows[term] + part
+    spread(2, 0, rows)
+    spread(1, 1, [square, ww, wb])
     for copy in arriving.values():
         copy.wait_send()
-    for number in range(2):
-        for phase in range(2):
-            all_landed(number, phase).wait_send()
+    all_landed(0, 0).wait_send()
+    all_landed(1, 0).wait_send()
     spread(2, 1, gather(2, 0, 4)[:3])
+
+    all_landed(1, 1).wait_recv()
+    theirs = [(landed_1[1, slot, 0:1], landed_1[1, slot, 1:2], landed_1[1, slot, 2:3]) for slot in range(len(groups[1]))]
+    theirs.append((square, ww, wb))
+    norm_square = functools.reduce(jnp.add, [b for b, _, _ in theirs])
+    inverse = 1.0 / jnp.sqrt(norm_square)
+    ratios = [inverse / shrink_of(b) for b, _, _ in theirs]
+    whole_ww = functools.reduce(jnp.add, [k * k * c for k, (_, c, _) in zip(ratios, theirs)])
+    whole_wb = functools.reduce(jnp.add, [k * k * d for k, (_, _, d) in zip(ratios, theirs)])
+    scale = 1.0 / jnp.sqrt(whole_ww)
+    extras = [scale / extra_of(c) for _, c, _ in theirs]
+    once = [k * k * e for k, e in zip(ratios, extras)]
+    twice = [k * e for k, e in zip(once, extras)]
     all_landed(2, 0).wait_send()
-    wq, qq, bq = gather(2, 1, 3)
-    wb = wb * scale
+    all_landed(1, 1).wait_send()
+
+    all_landed(2, 1).wait_recv()
+    last = [landed_2[1, slot] for slot in range(len(groups[1]))] + [mine_2[1]]
+    wq = functools.reduce(jnp.add, [k * part[0:1] for k, part in zip(once, last)])
+    qq = functools.reduce(jnp.add, [k * part[1:2] for k, part in zip(twice, last)])
+    bq = functools.reduce(jnp.add, [k * part[2:3] for k, part in zip(once, last)])
+    wq = wq * scale
+    wb = whole_wb * scale
     second = (bq - wq * wb) / (qq - wq * wq)
     weight_1 = (wb - wq * second) * scale
     weight_2 = second * scale
@@ -291,6 +341,7 @@
                 pltpu.VMEM(field, F32),
                 pltpu.VMEM(field, F32),
                 pltpu.VMEM(field, F32),
+                pltpu.VMEM(field, F32),
                 *[pltpu.VMEM((2, terms, cases), F32) for terms in TERMS],
                 *[pltpu.VMEM((2, others, terms, cases), F32) for terms in TERMS],
                 sem((5,)),
@@ -298,6 +349,7 @@
                 sem((4, 8)),
                 sem((len(TERMS), 2)),
                 sem((len(TERMS), 2)),
+                pltpu.SemaphoreType.REGULAR((2,)),
             ],
             compiler_params=pltpu.CompilerParams(
                 collective_id=0, has_side_effects=True, vmem_limit_bytes=48 * 1024 * 1024

time: 43.9 us -> 40.5 us (0.923)
  Pallas kernels: 43 us -> 39.7 us
    pallas_call x1, Pallas kernels: 43 us -> 39.7 us  [local(): pl.pallas_call(functools.partial(kernel, ngx, ngy, fast), out_shape=jax.S...]
where the time goes in v3:
time: 40.5 us; the launch traced here: 40.4 us
  Pallas kernels  39.7 us (98%)
  local copies, waits for them, and re-layouts  0.75 us (2%)
    pallas_call x1, Pallas kernels, local(): pl.pallas_call(functools.partial(kernel, ngx, ngy, fast), out_shape=jax.S...  39.7 us

profile of v3, /device:TPU:1, one launch (start us, length us, event | category | flops | bytes accessed | tf_op | source)
XLA Modules:
  0.0 40.4 jit_solution(7321087547327854725)
XLA Ops:
  0.0 39.7 %shard_map.28 = f32[2,2,192,128]{3,2,1,0:T(8,128)S(1)} custom-call(f32[2,2,192,128]{3,2,1,0:T(8,128)} %load_ref.1, bf16[4,2,2,192,192]{4,3,2,1,0:T(8,128)(2,1)} %blocks_ref.1), custom_call_target="tpu_custom_call" | custom-call | tf_op jit(solution)/shard_map/pallas_call | solution.py:325
  39.7 0.7 %copy.4 = f32[2,2,192,128]{3,2,1,0:T(8,128)} copy(f32[2,2,192,128]{3,2,1,0:T(8,128)S(1)} %shard_map.28) | data formatting | bytes 786432

commit v4 on v3

v4 whole, which is shorter than its diff:
```python
import functools

import jax
import jax.numpy as jnp
from jax import lax
from jax.experimental import pallas as pl
from jax.experimental.pallas import tpu as pltpu
from jax.sharding import PartitionSpec as P

MESH = pl.DeviceIdType.MESH
F32 = jnp.float32
BF16 = jnp.bfloat16
NODES = [(0, 0), (1, 0), (0, 1), (1, 1)]
EVEN, ODD = [(0, 0), (1, 0)], [(0, 1), (1, 1)]
PAIRS = [[[(0, 0)], [(1, 0)], [(0, 1)], [(1, 1)]]] * 5
XL, XH, YL, YH = range(4)
TERMS = (4, 4)


def dot(a, b):
    return jnp.dot(a, b, preferred_element_type=F32)


def split(u):
    high = u.astype(BF16)
    return high, (u - high.astype(F32)).astype(BF16)


def dot2(a, u):
    both = dot(a, jnp.concatenate(split(u), axis=1))
    half = u.shape[1]
    return both[:, :half] + both[:, half:]


def shrink_of(square):
    return jnp.where(square > 0.0, jnp.minimum(1.0 / jnp.sqrt(square), 1e12), 1.0)


def extra_of(square):
    return jnp.where(square > 0.0, jnp.minimum(1.0 / jnp.sqrt(square), 1e12), 1e-8)


def fold(a):
    return jnp.sum(a.reshape(-1, 8, a.shape[1]), axis=0)


def over_rows(a):
    return jnp.sum(a, axis=0, keepdims=True)


def kernel(
    ngx, ngy, fast,
    load_ref, blocks_ref, out_ref,
    v, m, t1, t2, reach, lift, up_base, sent, products, halo, first, total, c1, c2, w, scaled_w, scaled_v,
    mine_0, mine_1, landed_0, landed_1,
    load_sem, halo_send, halo_recv, sum_send, sum_recv, circle,
):
    gx, gy = lax.axis_index("gx"), lax.axis_index("gy")
    up_x, down_x = lax.rem(gx + 1, ngx), lax.rem(gx + ngx - 1, ngx)
    up_y, down_y = lax.rem(gy + 1, ngy), lax.rem(gy + ngy - 1, ngy)
    sides = {XL: (up_x, gy), XH: (down_x, gy), YL: (gx, up_y), YH: (gx, down_y)}
    has_up_x, has_down_x, has_up_y, has_down_y = gx < ngx - 1, gx > 0, gy < ngy - 1, gy > 0
    leaves = {XL: has_up_x, XH: has_down_x, YL: has_up_y, YH: has_down_y}
    arrives = {XL: has_down_x, XH: has_up_x, YL: has_down_y, YH: has_up_y}

    shape = (ngx // fast, fast, ngy // 2, 2)
    z, y, x, core = gx // fast, gx % fast, gy // 2, gy % 2
    chip = x

    def device(offset):
        dz, dy, dx, dc = offset
        return (
            lax.rem(z + dz, shape[0]) * fast + lax.rem(y + dy, shape[1]),
            lax.rem(x + dx, shape[2]) * 2 + lax.rem(core + dc, 2),
        )

    def offsets(*steps):
        wrapped = [tuple(d % n for d, n in zip(step, shape)) for step in steps]
        return [step for step in dict.fromkeys(wrapped) if any(step)]

    def hops(offset):
        return sum(min(d, n - d) for d, n in zip(offset, shape))

    ranges = [range(n) for n in shape]
    groups = [
        [device(step) for step in sorted(offsets(*steps), key=hops, reverse=True)]
        for steps in (
            [(dz, 0, 0, dc) for dz in ranges[0] for dc in ranges[3]],
            [(0, dy, dx, 0) for dy in ranges[1] for dx in ranges[2]],
        )
    ]
    def circle_of(*steps):
        wrapped = [(a % ngx, b % ngy) for a, b in steps]
        return [
            (lax.rem(gx + a, ngx), lax.rem(gy + b, ngy)) for a, b in dict.fromkeys(wrapped) if a or b
        ]

    circles = [
        circle_of((1, 0), (-1, 0), (0, 1), (0, -1)),
        circle_of((2, 0), (-2, 0), (0, 2), (0, -2)),
        circle_of((4, 0), (-4, 0), (0, 4)),
        circle_of((8, 0), (-8, 0)),
        [(gx, chip * 2 + 1 - core)],
    ]

    def tell(number):
        for partner in circles[number]:
            pl.semaphore_signal(circle.at[number], inc=1, device_id=partner, device_id_type=MESH)

    def hear(number):
        if circles[number]:
            pl.semaphore_wait(circle.at[number], len(circles[number]))

    mine = [mine_0, mine_1]
    landed = [landed_0, landed_1]

    barrier = pltpu.get_barrier_semaphore()
    for partner in sides.values():
        pl.semaphore_signal(barrier, inc=1, device_id=partner, device_id_type=MESH)

    loads = [
        pltpu.make_async_copy(load_ref, v, load_sem.at[0]),
        pltpu.make_async_copy(blocks_ref.at[3], m.at[3], load_sem.at[1]),
        pltpu.make_async_copy(blocks_ref.at[1], m.at[1], load_sem.at[2]),
        pltpu.make_async_copy(blocks_ref.at[2], m.at[2], load_sem.at[3]),
        pltpu.make_async_copy(blocks_ref.at[0], m.at[0], load_sem.at[4]),
    ]
    for copy in loads:
        copy.start()

    arriving = {}

    def send(source, step, side, place):
        slot = side * 2 + place
        copy = pltpu.make_async_remote_copy(
            src_ref=source,
            dst_ref=halo.at[step, side, place],
            send_sem=halo_send.at[step, slot],
            recv_sem=halo_recv.at[step, slot],
            device_id=sides[side],
            device_id_type=MESH,
        )
        pl.when(leaves[side])(copy.start)
        arriving[step, side, place] = copy

    def announce(step, i, j):
        if i == 0:
            send(sent.at[step, i, j], step, XH, j)
        if j == 0:
            send(sent.at[step, i, j], step, YH, i)

    def ups(pair):
        return [(0, j, 1, j) for i, j in pair if i == 1] + [(1, i, i, 1) for i, j in pair if j == 1]

    def upward(axis, i, j):
        return t2[i, j] if axis else t1[i, j]

    def pass_up(step, pair, values):
        for (axis, k, i, j), value in zip(ups(pair), values):
            products[step, axis, k] = value.astype(BF16)
        for axis, k, i, j in ups(pair):
            send(products.at[step, axis, k], step, YL if axis else XL, k)

    def reach_of(i, j):
        return [reach[0, j] if i else m[3, i, j], reach[1, i] if j else m[3, i, j]]

    def halos(step, i, j):
        return [halo[step, XH if i else XL, j], halo[step, YH if j else YL, i]]

    def through(matrices, step, i, j):
        across_x, across_y = halos(step, i, j)
        return dot(matrices[0], across_x) + dot(matrices[1], across_y)

    def prepare(field, base):
        for i, j in NODES:
            field[i, j] = base(i, j)
        for axis, k, i, j in ups(NODES):
            up_base[axis, k] = dot(upward(axis, i, j), field[i, j].astype(BF16))

    def exchange(step, field, sign):
        for pair in PAIRS[step]:
            for i, j in pair:
                land(step - 1, i, j)
            for i, j in pair:
                value = field[i, j] + sign * through(reach_of(i, j), step - 1, i, j)
                field[i, j] = value
                sent[step, i, j] = value.astype(BF16)
            values = [
                up_base[axis, k] + sign * through([lift[axis, 0, k], lift[axis, 1, k]], step - 1, i, j)
                for axis, k, i, j in ups(pair)
            ]
            for i, j in pair:
                announce(step, i, j)
            pass_up(step, pair, values)

    def inner(step, field):
        for i, j in NODES:
            value = dot2(m[0, i, j], field[i, j]) if step < 3 else dot(m[0, i, j], sent[step, i, j])
            value += dot(m[1, 0, j], sent[step, 1, j]) if i == 0 else dot(t1[0, j], sent[step, 0, j])
            value += dot(m[2, i, 0], sent[step, i, 1]) if j == 0 else dot(t2[i, 0], sent[step, i, 0])
            total[i, j] = value

    def land(step, i, j):
        for side, place in ((YH if j else YL, i), (XH if i else XL, j)):
            pl.when(arrives[side])(arriving[step, side, place].wait_recv)

    def outer(step, i, j):
        value = total[i, j]
        value += dot(m[2, i, 1], halo[step, YH, i]) if j else halo[step, YL, i].astype(F32)
        value += dot(m[1, 1, j], halo[step, XH, j]) if i else halo[step, XL, j].astype(F32)
        return value

    def spread(number, phase, rows):
        term = 0
        for row in rows:
            mine[number][phase, pl.ds(term, row.shape[0])] = row
            term += row.shape[0]
        for slot, partner in enumerate(groups[phase]):
            pltpu.make_async_remote_copy(
                src_ref=mine[number].at[phase],
                dst_ref=landed[number].at[phase, slot],
                send_sem=sum_send.at[number, phase],
                recv_sem=sum_recv.at[number, phase],
                device_id=partner,
                device_id_type=MESH,
            ).start()

    def all_landed(number, phase):
        return pltpu.make_async_remote_copy(
            src_ref=landed[number].at[phase],
            dst_ref=landed[number].at[phase],
            send_sem=sum_send.at[number, phase],
            recv_sem=sum_recv.at[number, phase],
            device_id=groups[phase][0],
            device_id_type=MESH,
        )

    def joined(parts, to=shrink_of):
        square = functools.reduce(jnp.add, [part[0:1] for part in parts])
        ratios = [to(square) / shrink_of(part[0:1]) for part in parts]
        others = [
            functools.reduce(jnp.add, [k * k * part[term : term + 1] for k, part in zip(ratios, parts)])
            for term in (1, 2)
        ]
        return [square, *others], ratios

    def inner_products(*pairs):
        rows = [None] * len(pairs)
        for i, j in NODES:
            for term, (a, b) in enumerate(pairs):
                part = fold(a[i, j] * b[i, j])
                rows[term] = part if rows[term] is None else rows[term] + part
        return [over_rows(row) for row in rows]

    for side in sides:

        @pl.when(jnp.logical_not(arrives[side]))
        def _():
            for step in range(4):
                halo[step, side] = jnp.zeros(halo.shape[2:], BF16)

    mine_0[...] = jnp.zeros(mine_0.shape, F32)
    mine_1[...] = jnp.zeros(mine_1.shape, F32)

    loads[0].wait()
    loads[1].wait()
    for i, j in NODES:
        value = dot2(m[3, i, j], v[i, j])
        first[i, j] = value
        sent[0, i, j] = value.astype(BF16)
    pl.semaphore_wait(barrier, len(sides))
    for i, j in EVEN + ODD:
        announce(0, i, j)
    tell(0)
    loads[2].wait()
    loads[3].wait()

    for k in range(2):
        t1[1, k] = m[1, 1, k].T
    for k in range(2):
        t2[k, 1] = m[2, k, 1].T
    pass_up(0, NODES, [dot(upward(axis, i, j), sent[0, i, j]) for axis, k, i, j in ups(NODES)])
    for k in range(2):
        t1[0, k] = m[1, 0, k].T
        t2[k, 0] = m[2, k, 0].T
    loads[4].wait()
    inner(0, first)
    for k in range(2):
        reach[0, k] = dot(m[3, 1, k], m[1, 1, k]).astype(BF16)
        reach[1, k] = dot(m[3, k, 1], m[2, k, 1]).astype(BF16)
    for axis, k, i, j in ups(NODES):
        for side, matrix in enumerate(reach_of(i, j)):
            lift[axis, side, k] = dot(upward(axis, i, j), matrix).astype(BF16)
    prepare(c1, lambda i, j: first[i, j] + dot2(m[3, i, j], v[i, j] - total[i, j]))
    hear(0)
    tell(1)

    exchange(1, c1, -1.0)
    hear(1)
    tell(2)
    inner(1, c1)
    prepare(first, lambda i, j: dot2(m[3, i, j], total[i, j]))
    (square,) = inner_products((v, v))
    shrink = shrink_of(square)
    for i, j in NODES:
        scaled_v[i, j] = v[i, j] * shrink
    hear(2)
    tell(3)

    exchange(2, first, 1.0)
    for i, j in NODES:
        w[i, j] = outer(1, i, j)
    inner(2, first)
    prepare(c2, lambda i, j: first[i, j] + dot2(m[3, i, j], w[i, j] - total[i, j]))
    for i, j in NODES:
        scaled_w[i, j] = w[i, j] * shrink
    sums = [square, *inner_products((scaled_w, scaled_w), (scaled_w, scaled_v))]
    hear(3)
    tell(4)
    hear(4)
    spread(0, 0, sums)

    exchange(3, c2, -1.0)
    inner(3, c2)
    all_landed(0, 0).wait_recv()
    group, ratios = joined([mine_0[0], *[landed_0[0, slot] for slot in range(len(groups[0]))]])
    square_of_group, ww, wb = group
    extra = extra_of(ww)
    whole_shrink = shrink_of(square_of_group)
    both = whole_shrink * extra
    ratio = whole_shrink / shrink
    rows = [None] * 3
    for i, j in EVEN + ODD:
        land(3, i, j)
        unit_q = outer(3, i, j) * both
        for term, other in enumerate((scaled_w[i, j], unit_q, scaled_v[i, j])):
            part = fold(other * unit_q)
            rows[term] = part if rows[term] is None else rows[term] + part
    rows = [over_rows(row) for row in rows]
    spread(1, 0, [rows[0] * ratio, rows[1], rows[2] * ratio])
    spread(0, 1, group)
    for (_, side, _), copy in arriving.items():
        pl.when(leaves[side])(copy.wait_send)
    all_landed(0, 0).wait_send()
    all_landed(1, 0).wait_recv()
    spread(1, 1, [functools.reduce(jnp.add, [mine_1[0], *[landed_1[0, slot] for slot in range(len(groups[0]))]])])

    all_landed(0, 1).wait_recv()
    theirs = [mine_0[1], *[landed_0[1, slot] for slot in range(len(groups[1]))]]
    (_, whole_ww, whole_wb), ratios = joined(theirs, lambda square: 1.0 / jnp.sqrt(square))
    scale = 1.0 / jnp.sqrt(whole_ww)
    extras = [scale / extra_of(part[1:2]) for part in theirs]
    once = [k * k * e for k, e in zip(ratios, extras)]
    twice = [k * e for k, e in zip(once, extras)]
    all_landed(1, 0).wait_send()
    all_landed(0, 1).wait_send()

    all_landed(1, 1).wait_recv()
    last = [mine_1[1], *[landed_1[1, slot] for slot in range(len(groups[1]))]]
    wq = functools.reduce(jnp.add, [k * part[0:1] for k, part in zip(once, last)])
    qq = functools.reduce(jnp.add, [k * part[1:2] for k, part in zip(twice, last)])
    bq = functools.reduce(jnp.add, [k * part[2:3] for k, part in zip(once, last)])
    wq = wq * scale
    wb = whole_wb * scale
    second = (bq - wq * wb) / (qq - wq * wq)
    weight_1 = (wb - wq * second) * scale
    weight_2 = second * scale
    for i, j in NODES:
        out_ref[i, j] = weight_1 * c1[i, j] + weight_2 * c2[i, j]
    all_landed(1, 1).wait_send()


def solution(mesh):
    ngx, ngy = mesh.shape["gx"], mesh.shape["gy"]
    fast = 4
    others = 2 * (ngx // fast) - 1

    def local(load_vector, blocks):
        cx, cy, size, cases = load_vector.shape
        field = (cx, cy, size, cases)
        matrices = (cx, cy, size, size)
        sem = pltpu.SemaphoreType.DMA
        return pl.pallas_call(
            functools.partial(kernel, ngx, ngy, fast),
            out_shape=jax.ShapeDtypeStruct(field, F32),
            in_specs=[pl.BlockSpec(memory_space=pltpu.HBM)] * 2,
            out_specs=pl.BlockSpec(memory_space=pltpu.VMEM),
            scratch_shapes=[
                pltpu.VMEM(field, F32),
                pltpu.VMEM((4, *matrices), BF16),
                pltpu.VMEM(matrices, BF16),
                pltpu.VMEM(matrices, BF16),
                pltpu.VMEM((2, 2, size, size), BF16),
                pltpu.VMEM((2, 2, 2, size, size), BF16),
                pltpu.VMEM((2, 2, size, cases), F32),
                pltpu.VMEM((4, *field), BF16),
                pltpu.VMEM((4, 2, 2, size, cases), BF16),
                pltpu.VMEM((4, 4, 2, size, cases), BF16),
                pltpu.VMEM(field, F32),
                pltpu.VMEM(field, F32),
                pltpu.VMEM(field, F32),
                pltpu.VMEM(field, F32),
                pltpu.VMEM(field, F32),
                pltpu.VMEM(field, F32),
                pltpu.VMEM(field, F32),
                *[pltpu.VMEM((2, terms, cases), F32) for terms in TERMS],
                *[pltpu.VMEM((2, others, terms, cases), F32) for terms in TERMS],
                sem((5,)),
                sem((4, 8)),
                sem((4, 8)),
                sem((len(TERMS), 2)),
                sem((len(TERMS), 2)),
                pltpu.SemaphoreType.REGULAR((5,)),
            ],
            compiler_params=pltpu.CompilerParams(
                collective_id=0, has_side_effects=True, vmem_limit_bytes=48 * 1024 * 1024
            ),
        )(*[pltpu.with_memory_space_constraint(a, pltpu.HBM) for a in (load_vector, blocks)])

    return jax.shard_map(
        local,
        mesh=mesh,
        in_specs=(P("gx", "gy", None, None), P(None, "gx", "gy", None, None)),
        out_specs=P("gx", "gy", None, None),
        check_vma=False,
    )
```

time: 40.5 us -> 38.9 us (0.960)
  Pallas kernels: 39.7 us -> 38 us
    pallas_call x1, Pallas kernels: 39.7 us -> 38 us  [local(): pl.pallas_call(functools.partial(kernel, ngx, ngy, fast), out_shape=jax.S...]
where the time goes in v4:
time: 38.9 us; the launch traced here: 38.8 us
  Pallas kernels  38 us (98%)
  local copies, waits for them, and re-layouts  0.75 us (2%)
    pallas_call x1, Pallas kernels, local(): pl.pallas_call(functools.partial(kernel, ngx, ngy, fast), out_shape=jax.S...  38 us

profile of v4, /device:TPU:1, one launch (start us, length us, event | category | flops | bytes accessed | tf_op | source)
XLA Modules:
  0.0 38.8 jit_solution(6071578320727403753)
XLA Ops:
  0.0 38.0 %shard_map.28 = f32[2,2,192,128]{3,2,1,0:T(8,128)S(1)} custom-call(f32[2,2,192,128]{3,2,1,0:T(8,128)} %load_ref.1, bf16[4,2,2,192,192]{4,3,2,1,0:T(8,128)(2,1)} %blocks_ref.1), custom_call_target="tpu_custom_call" | custom-call | tf_op jit(solution)/shard_map/pallas_call | solution.py:383
  38.0 0.7 %copy.4 = f32[2,2,192,128]{3,2,1,0:T(8,128)} copy(f32[2,2,192,128]{3,2,1,0:T(8,128)S(1)} %shard_map.28) | data formatting | bytes 786432

commit v5 on v4

--- a/solution.py
+++ b/solution.py
@@ -14,7 +14,7 @@
 EVEN, ODD = [(0, 0), (1, 0)], [(0, 1), (1, 1)]
 PAIRS = [[[(0, 0)], [(1, 0)], [(0, 1)], [(1, 1)]]] * 5
 XL, XH, YL, YH = range(4)
-TERMS = (4, 4)
+TERMS = 4
 
 
 def dot(a, b):
@@ -52,7 +52,7 @@
     ngx, ngy, fast,
     load_ref, blocks_ref, out_ref,
     v, m, t1, t2, reach, lift, up_base, sent, products, halo, first, total, c1, c2, w, scaled_w, scaled_v,
-    mine_0, mine_1, landed_0, landed_1,
+    mine, landed,
     load_sem, halo_send, halo_recv, sum_send, sum_recv, circle,
 ):
     gx, gy = lax.axis_index("gx"), lax.axis_index("gy")
@@ -111,8 +111,6 @@
         if circles[number]:
             pl.semaphore_wait(circle.at[number], len(circles[number]))
 
-    mine = [mine_0, mine_1]
-    landed = [landed_0, landed_1]
 
     barrier = pltpu.get_barrier_semaphore()
     for partner in sides.values():
@@ -131,12 +129,11 @@
     arriving = {}
 
     def send(source, step, side, place):
-        slot = side * 2 + place
         copy = pltpu.make_async_remote_copy(
             src_ref=source,
-            dst_ref=halo.at[step, side, place],
-            send_sem=halo_send.at[step, slot],
-            recv_sem=halo_recv.at[step, slot],
+            dst_ref=halo.at[side, step, place],
+            send_sem=halo_send.at[side],
+            recv_sem=halo_recv.at[step % 2, side * 2 + place],
             device_id=sides[side],
             device_id_type=MESH,
         )
@@ -165,7 +162,7 @@
         return [reach[0, j] if i else m[3, i, j], reach[1, i] if j else m[3, i, j]]
 
     def halos(step, i, j):
-        return [halo[step, XH if i else XL, j], halo[step, YH if j else YL, i]]
+        return [halo[XH if i else XL, step, j], halo[YH if j else YL, step, i]]
 
     def through(matrices, step, i, j):
         across_x, across_y = halos(step, i, j)
@@ -206,34 +203,35 @@
 
     def outer(step, i, j):
         value = total[i, j]
-        value += dot(m[2, i, 1], halo[step, YH, i]) if j else halo[step, YL, i].astype(F32)
-        value += dot(m[1, 1, j], halo[step, XH, j]) if i else halo[step, XL, j].astype(F32)
+        value += dot(m[2, i, 1], halo[YH, step, i]) if j else halo[YL, step, i].astype(F32)
+        value += dot(m[1, 1, j], halo[XH, step, j]) if i else halo[XL, step, j].astype(F32)
         return value
 
     def spread(number, phase, rows):
         term = 0
         for row in rows:
-            mine[number][phase, pl.ds(term, row.shape[0])] = row
+            mine[number, phase, pl.ds(term, row.shape[0])] = row
             term += row.shape[0]
         for slot, partner in enumerate(groups[phase]):
             pltpu.make_async_remote_copy(
-                src_ref=mine[number].at[phase],
-                dst_ref=landed[number].at[phase, slot],
-                send_sem=sum_send.at[number, phase],
+                src_ref=mine.at[number, phase],
+                dst_ref=landed.at[number, phase, slot],
+                send_sem=sum_send.at[0],
                 recv_sem=sum_recv.at[number, phase],
                 device_id=partner,
                 device_id_type=MESH,
             ).start()
 
-    def all_landed(number, phase):
-        return pltpu.make_async_remote_copy(
-            src_ref=landed[number].at[phase],
-            dst_ref=landed[number].at[phase],
-            send_sem=sum_send.at[number, phase],
+    def arrive(number, phase):
+        pltpu.make_async_remote_copy(
+            src_ref=landed.at[number, phase],
+            dst_ref=landed.at[number, phase],
+            send_sem=sum_send.at[0],
             recv_sem=sum_recv.at[number, phase],
             device_id=groups[phase][0],
             device_id_type=MESH,
-        )
+        ).wait_recv()
+        return [mine[number, phase], *[landed[number, phase, slot] for slot in range(len(groups[phase]))]]
 
     def joined(parts, to=shrink_of):
         square = functools.reduce(jnp.add, [part[0:1] for part in parts])
@@ -256,11 +254,9 @@
 
         @pl.when(jnp.logical_not(arrives[side]))
         def _():
-            for step in range(4):
-                halo[step, side] = jnp.zeros(halo.shape[2:], BF16)
-
-    mine_0[...] = jnp.zeros(mine_0.shape, F32)
-    mine_1[...] = jnp.zeros(mine_1.shape, F32)
+            halo[side] = jnp.zeros(halo.shape[1:], BF16)
+
+    mine[...] = jnp.zeros(mine.shape, F32)
 
     loads[0].wait()
     loads[1].wait()
@@ -322,8 +318,7 @@
 
     exchange(3, c2, -1.0)
     inner(3, c2)
-    all_landed(0, 0).wait_recv()
-    group, ratios = joined([mine_0[0], *[landed_0[0, slot] for slot in range(len(groups[0]))]])
+    group, _ = joined(arrive(0, 0))
     square_of_group, ww, wb = group
     extra = extra_of(ww)
     whole_shrink = shrink_of(square_of_group)
@@ -339,24 +334,26 @@
     rows = [over_rows(row) for row in rows]
     spread(1, 0, [rows[0] * ratio, rows[1], rows[2] * ratio])
     spread(0, 1, group)
-    for (_, side, _), copy in arriving.items():
-        pl.when(leaves[side])(copy.wait_send)
-    all_landed(0, 0).wait_send()
-    all_landed(1, 0).wait_recv()
-    spread(1, 1, [functools.reduce(jnp.add, [mine_1[0], *[landed_1[0, slot] for slot in range(len(groups[0]))]])])
-
-    all_landed(0, 1).wait_recv()
-    theirs = [mine_0[1], *[landed_0[1, slot] for slot in range(len(groups[1]))]]
+    for side, partner in sides.items():
+        all_sent = pltpu.make_async_remote_copy(
+            src_ref=halo.at[side],
+            dst_ref=halo.at[side],
+            send_sem=halo_send.at[side],
+            recv_sem=halo_recv.at[0, side],
+            device_id=partner,
+            device_id_type=MESH,
+        )
+        pl.when(leaves[side])(all_sent.wait_send)
+    spread(1, 1, [functools.reduce(jnp.add, arrive(1, 0))])
+
+    theirs = arrive(0, 1)
     (_, whole_ww, whole_wb), ratios = joined(theirs, lambda square: 1.0 / jnp.sqrt(square))
     scale = 1.0 / jnp.sqrt(whole_ww)
     extras = [scale / extra_of(part[1:2]) for part in theirs]
     once = [k * k * e for k, e in zip(ratios, extras)]
     twice = [k * e for k, e in zip(once, extras)]
-    all_landed(1, 0).wait_send()
-    all_landed(0, 1).wait_send()
-
-    all_landed(1, 1).wait_recv()
-    last = [mine_1[1], *[landed_1[1, slot] for slot in range(len(groups[1]))]]
+
+    last = arrive(1, 1)
     wq = functools.reduce(jnp.add, [k * part[0:1] for k, part in zip(once, last)])
     qq = functools.reduce(jnp.add, [k * part[1:2] for k, part in zip(twice, last)])
     bq = functools.reduce(jnp.add, [k * part[2:3] for k, part in zip(once, last)])
@@ -367,7 +364,14 @@
     weight_2 = second * scale
     for i, j in NODES:
         out_ref[i, j] = weight_1 * c1[i, j] + weight_2 * c2[i, j]
-    all_landed(1, 1).wait_send()
+    pltpu.make_async_remote_copy(
+        src_ref=landed,
+        dst_ref=landed,
+        send_sem=sum_send.at[0],
+        recv_sem=sum_recv.at[0, 0],
+        device_id=groups[0][0],
+        device_id_type=MESH,
+    ).wait_send()
 
 
 def solution(mesh):
@@ -403,13 +407,13 @@
                 pltpu.VMEM(field, F32),
                 pltpu.VMEM(field, F32),
                 pltpu.VMEM(field, F32),
-                *[pltpu.VMEM((2, terms, cases), F32) for terms in TERMS],
-                *[pltpu.VMEM((2, others, terms, cases), F32) for terms in TERMS],
+                pltpu.VMEM((2, 2, TERMS, cases), F32),
+                pltpu.VMEM((2, 2, others, TERMS, cases), F32),
                 sem((5,)),
-                sem((4, 8)),
-                sem((4, 8)),
-                sem((len(TERMS), 2)),
-                sem((len(TERMS), 2)),
+                sem((4,)),
+                sem((2, 8)),
+                sem((1,)),
+                sem((2, 2)),
                 pltpu.SemaphoreType.REGULAR((5,)),
             ],
             compiler_params=pltpu.CompilerParams(

time: 38.9 us -> 38.4 us (0.987)
  Pallas kernels: 38 us -> 37.6 us
    pallas_call x1, Pallas kernels: 38 us -> 37.6 us  [local(): pl.pallas_call(functools.partial(kernel, ngx, ngy, fast), out_shape=jax.S...]
where the time goes in v5:
time: 38.4 us; the launch traced here: 38.3 us
  Pallas kernels  37.6 us (98%)
  local copies, waits for them, and re-layouts  0.75 us (2%)
    pallas_call x1, Pallas kernels, local(): pl.pallas_call(functools.partial(kernel, ngx, ngy, fast), out_shape=jax.S...  37.6 us

profile of v5, /device:TPU:1, one launch (start us, length us, event | category | flops | bytes accessed | tf_op | source)
XLA Modules:
  0.0 38.3 jit_solution(3146836784718358482)
XLA Ops:
  0.0 37.6 %shard_map.28 = f32[2,2,192,128]{3,2,1,0:T(8,128)S(1)} custom-call(f32[2,2,192,128]{3,2,1,0:T(8,128)} %load_ref.1, bf16[4,2,2,192,192]{4,3,2,1,0:T(8,128)(2,1)} %blocks_ref.1), custom_call_target="tpu_custom_call" | custom-call | tf_op jit(solution)/shard_map/pallas_call | solution.py:387
  37.6 0.7 %copy.4 = f32[2,2,192,128]{3,2,1,0:T(8,128)} copy(f32[2,2,192,128]{3,2,1,0:T(8,128)S(1)} %shard_map.28) | data formatting | bytes 786432

commit v6 on v5

--- a/solution.py
+++ b/solution.py
@@ -14,6 +14,7 @@
 EVEN, ODD = [(0, 0), (1, 0)], [(0, 1), (1, 1)]
 PAIRS = [[[(0, 0)], [(1, 0)], [(0, 1)], [(1, 1)]]] * 5
 XL, XH, YL, YH = range(4)
+SLOTS = [(XL, 0), (XL, 1), (XH, 0), (XH, 1), (YL, None), (YH, None)]
 TERMS = 4
 
 
@@ -78,12 +79,9 @@
         wrapped = [tuple(d % n for d, n in zip(step, shape)) for step in steps]
         return [step for step in dict.fromkeys(wrapped) if any(step)]
 
-    def hops(offset):
-        return sum(min(d, n - d) for d, n in zip(offset, shape))
-
-    ranges = [range(n) for n in shape]
+    ranges = [{8: (5, 4, 3, 2, 1, 6, 7, 0), 4: (1, 2, 3, 0), 2: (1, 0)}.get(n, range(n)) for n in shape]
     groups = [
-        [device(step) for step in sorted(offsets(*steps), key=hops, reverse=True)]
+        [device(step) for step in offsets(*steps)]
         for steps in (
             [(dz, 0, 0, dc) for dz in ranges[0] for dc in ranges[3]],
             [(0, dy, dx, 0) for dy in ranges[1] for dx in ranges[2]],
@@ -119,21 +117,21 @@
     loads = [
         pltpu.make_async_copy(load_ref, v, load_sem.at[0]),
         pltpu.make_async_copy(blocks_ref.at[3], m.at[3], load_sem.at[1]),
-        pltpu.make_async_copy(blocks_ref.at[1], m.at[1], load_sem.at[2]),
-        pltpu.make_async_copy(blocks_ref.at[2], m.at[2], load_sem.at[3]),
-        pltpu.make_async_copy(blocks_ref.at[0], m.at[0], load_sem.at[4]),
+        pltpu.make_async_copy(blocks_ref.at[pl.ds(1, 2)], m.at[pl.ds(1, 2)], load_sem.at[2]),
+        pltpu.make_async_copy(blocks_ref.at[0], m.at[0], load_sem.at[3]),
     ]
     for copy in loads:
         copy.start()
 
     arriving = {}
 
-    def send(source, step, side, place):
+    def send(source, step, side, place=None):
+        target = halo.at[side, step] if place is None else halo.at[side, step, place]
         copy = pltpu.make_async_remote_copy(
             src_ref=source,
-            dst_ref=halo.at[side, step, place],
+            dst_ref=target,
             send_sem=halo_send.at[side],
-            recv_sem=halo_recv.at[step % 2, side * 2 + place],
+            recv_sem=halo_recv.at[step % 2, SLOTS.index((side, place))],
             device_id=sides[side],
             device_id_type=MESH,
         )
@@ -142,9 +140,9 @@
 
     def announce(step, i, j):
         if i == 0:
-            send(sent.at[step, i, j], step, XH, j)
-        if j == 0:
-            send(sent.at[step, i, j], step, YH, i)
+            send(sent.at[step, j, i], step, XH, j)
+        if (i, j) == (1, 0):
+            send(sent.at[step, j], step, YH)
 
     def ups(pair):
         return [(0, j, 1, j) for i, j in pair if i == 1] + [(1, i, i, 1) for i, j in pair if j == 1]
@@ -156,7 +154,10 @@
         for (axis, k, i, j), value in zip(ups(pair), values):
             products[step, axis, k] = value.astype(BF16)
         for axis, k, i, j in ups(pair):
-            send(products.at[step, axis, k], step, YL if axis else XL, k)
+            if axis == 0:
+                send(products.at[step, 0, k], step, XL, k)
+            elif k == 1:
+                send(products.at[step, 1], step, YL)
 
     def reach_of(i, j):
         return [reach[0, j] if i else m[3, i, j], reach[1, i] if j else m[3, i, j]]
@@ -181,7 +182,7 @@
             for i, j in pair:
                 value = field[i, j] + sign * through(reach_of(i, j), step - 1, i, j)
                 field[i, j] = value
-                sent[step, i, j] = value.astype(BF16)
+                sent[step, j, i] = value.astype(BF16)
             values = [
                 up_base[axis, k] + sign * through([lift[axis, 0, k], lift[axis, 1, k]], step - 1, i, j)
                 for axis, k, i, j in ups(pair)
@@ -192,13 +193,16 @@
 
     def inner(step, field):
         for i, j in NODES:
-            value = dot2(m[0, i, j], field[i, j]) if step < 3 else dot(m[0, i, j], sent[step, i, j])
-            value += dot(m[1, 0, j], sent[step, 1, j]) if i == 0 else dot(t1[0, j], sent[step, 0, j])
-            value += dot(m[2, i, 0], sent[step, i, 1]) if j == 0 else dot(t2[i, 0], sent[step, i, 0])
+            value = dot2(m[0, i, j], field[i, j]) if step < 3 else dot(m[0, i, j], sent[step, j, i])
+            value += dot(m[1, 0, j], sent[step, j, 1]) if i == 0 else dot(t1[0, j], sent[step, j, 0])
+            value += dot(m[2, i, 0], sent[step, 1, i]) if j == 0 else dot(t2[i, 0], sent[step, 0, i])
             total[i, j] = value
 
     def land(step, i, j):
-        for side, place in ((YH if j else YL, i), (XH if i else XL, j)):
+        keys = [(XH if i else XL, j)]
+        if i == 0:
+            keys.append((YH if j else YL, None))
+        for side, place in keys:
             pl.when(arrives[side])(arriving[step, side, place].wait_recv)
 
     def outer(step, i, j):
@@ -234,13 +238,12 @@
         return [mine[number, phase], *[landed[number, phase, slot] for slot in range(len(groups[phase]))]]
 
     def joined(parts, to=shrink_of):
-        square = functools.reduce(jnp.add, [part[0:1] for part in parts])
-        ratios = [to(square) / shrink_of(part[0:1]) for part in parts]
-        others = [
-            functools.reduce(jnp.add, [k * k * part[term : term + 1] for k, part in zip(ratios, parts)])
-            for term in (1, 2)
-        ]
-        return [square, *others], ratios
+        squares, sizes, overlaps = (
+            jnp.concatenate([part[term : term + 1] for part in parts], axis=0) for term in range(3)
+        )
+        square = over_rows(squares)
+        ratios = to(square) / shrink_of(squares)
+        return [square, over_rows(ratios * ratios * sizes), over_rows(ratios * ratios * overlaps)], ratios, sizes
 
     def inner_products(*pairs):
         rows = [None] * len(pairs)
@@ -263,23 +266,22 @@
     for i, j in NODES:
         value = dot2(m[3, i, j], v[i, j])
         first[i, j] = value
-        sent[0, i, j] = value.astype(BF16)
+        sent[0, j, i] = value.astype(BF16)
     pl.semaphore_wait(barrier, len(sides))
     for i, j in EVEN + ODD:
         announce(0, i, j)
     tell(0)
     loads[2].wait()
-    loads[3].wait()
 
     for k in range(2):
         t1[1, k] = m[1, 1, k].T
     for k in range(2):
         t2[k, 1] = m[2, k, 1].T
-    pass_up(0, NODES, [dot(upward(axis, i, j), sent[0, i, j]) for axis, k, i, j in ups(NODES)])
+    pass_up(0, NODES, [dot(upward(axis, i, j), sent[0, j, i]) for axis, k, i, j in ups(NODES)])
     for k in range(2):
         t1[0, k] = m[1, 0, k].T
         t2[k, 0] = m[2, k, 0].T
-    loads[4].wait()
+    loads[3].wait()
     inner(0, first)
     for k in range(2):
         reach[0, k] = dot(m[3, 1, k], m[1, 1, k]).astype(BF16)
@@ -318,7 +320,7 @@
 
     exchange(3, c2, -1.0)
     inner(3, c2)
-    group, _ = joined(arrive(0, 0))
+    group, _, _ = joined(arrive(0, 0))
     square_of_group, ww, wb = group
     extra = extra_of(ww)
     whole_shrink = shrink_of(square_of_group)
@@ -347,16 +349,18 @@
     spread(1, 1, [functools.reduce(jnp.add, arrive(1, 0))])
 
     theirs = arrive(0, 1)
-    (_, whole_ww, whole_wb), ratios = joined(theirs, lambda square: 1.0 / jnp.sqrt(square))
+    (_, whole_ww, whole_wb), ratios, sizes = joined(theirs, lambda square: 1.0 / jnp.sqrt(square))
     scale = 1.0 / jnp.sqrt(whole_ww)
-    extras = [scale / extra_of(part[1:2]) for part in theirs]
-    once = [k * k * e for k, e in zip(ratios, extras)]
-    twice = [k * e for k, e in zip(once, extras)]
-
-    last = arrive(1, 1)
-    wq = functools.reduce(jnp.add, [k * part[0:1] for k, part in zip(once, last)])
-    qq = functools.reduce(jnp.add, [k * part[1:2] for k, part in zip(twice, last)])
-    bq = functools.reduce(jnp.add, [k * part[2:3] for k, part in zip(once, last)])
+    extras = scale / extra_of(sizes)
+    once = ratios * ratios * extras
+    twice = once * extras
+    factors = []
+    for k in range(len(theirs)):
+        row = once[k : k + 1]
+        factors.append(jnp.concatenate([row, twice[k : k + 1], row, row], axis=0))
+
+    last = functools.reduce(jnp.add, [factor * part for factor, part in zip(factors, arrive(1, 1))])
+    wq, qq, bq = last[0:1], last[1:2], last[2:3]
     wq = wq * scale
     wb = whole_wb * scale
     second = (bq - wq * wb) / (qq - wq * wq)
@@ -409,9 +413,9 @@
                 pltpu.VMEM(field, F32),
                 pltpu.VMEM((2, 2, TERMS, cases), F32),
                 pltpu.VMEM((2, 2, others, TERMS, cases), F32),
-                sem((5,)),
                 sem((4,)),
-                sem((2, 8)),
+                sem((4,)),
+                sem((2, len(SLOTS))),
                 sem((1,)),
                 sem((2, 2)),
                 pltpu.SemaphoreType.REGULAR((5,)),

time: 38.4 us -> 38.4 us (level)
  no operation moved by 1% of the time
where the time goes in v6:
time: 38.4 us; the launch traced here: 38.3 us
  Pallas kernels  37.5 us (98%)
  local copies, waits for them, and re-layouts  0.75 us (2%)
    pallas_call x1, Pallas kernels, local(): pl.pallas_call(functools.partial(kernel, ngx, ngy, fast), out_shape=jax.S...  37.5 us

profile of v6, /device:TPU:1, one launch (start us, length us, event | category | flops | bytes accessed | tf_op | source)
XLA Modules:
  0.0 38.3 jit_solution(4175916864298333615)
XLA Ops:
  0.0 37.5 %shard_map.28 = f32[2,2,192,128]{3,2,1,0:T(8,128)S(1)} custom-call(f32[2,2,192,128]{3,2,1,0:T(8,128)} %load_ref.1, bf16[4,2,2,192,192]{4,3,2,1,0:T(8,128)(2,1)} %blocks_ref.1), custom_call_target="tpu_custom_call" | custom-call | tf_op jit(solution)/shard_map/pallas_call | solution.py:391
  37.6 0.7 %copy.4 = f32[2,2,192,128]{3,2,1,0:T(8,128)} copy(f32[2,2,192,128]{3,2,1,0:T(8,128)S(1)} %shard_map.28) | data formatting | bytes 786432

commit v7 on v6

--- a/solution.py
+++ b/solution.py
@@ -11,8 +11,6 @@
 F32 = jnp.float32
 BF16 = jnp.bfloat16
 NODES = [(0, 0), (1, 0), (0, 1), (1, 1)]
-EVEN, ODD = [(0, 0), (1, 0)], [(0, 1), (1, 1)]
-PAIRS = [[[(0, 0)], [(1, 0)], [(0, 1)], [(1, 1)]]] * 5
 XL, XH, YL, YH = range(4)
 SLOTS = [(XL, 0), (XL, 1), (XH, 0), (XH, 1), (YL, None), (YH, None)]
 TERMS = 4
@@ -66,7 +64,6 @@
 
     shape = (ngx // fast, fast, ngy // 2, 2)
     z, y, x, core = gx // fast, gx % fast, gy // 2, gy % 2
-    chip = x
 
     def device(offset):
         dz, dy, dx, dc = offset
@@ -98,7 +95,7 @@
         circle_of((2, 0), (-2, 0), (0, 2), (0, -2)),
         circle_of((4, 0), (-4, 0), (0, 4)),
         circle_of((8, 0), (-8, 0)),
-        [(gx, chip * 2 + 1 - core)],
+        [(gx, x * 2 + 1 - core)],
     ]
 
     def tell(number):
@@ -176,20 +173,17 @@
             up_base[axis, k] = dot(upward(axis, i, j), field[i, j].astype(BF16))
 
     def exchange(step, field, sign):
-        for pair in PAIRS[step]:
-            for i, j in pair:
-                land(step - 1, i, j)
-            for i, j in pair:
-                value = field[i, j] + sign * through(reach_of(i, j), step - 1, i, j)
-                field[i, j] = value
-                sent[step, j, i] = value.astype(BF16)
+        for i, j in NODES:
+            land(step - 1, i, j)
+            value = field[i, j] + sign * through(reach_of(i, j), step - 1, i, j)
+            field[i, j] = value
+            sent[step, j, i] = value.astype(BF16)
             values = [
                 up_base[axis, k] + sign * through([lift[axis, 0, k], lift[axis, 1, k]], step - 1, i, j)
-                for axis, k, i, j in ups(pair)
+                for axis, k, i, j in ups([(i, j)])
             ]
-            for i, j in pair:
-                announce(step, i, j)
-            pass_up(step, pair, values)
+            announce(step, i, j)
+            pass_up(step, [(i, j)], values)
 
     def inner(step, field):
         for i, j in NODES:
@@ -268,7 +262,7 @@
         first[i, j] = value
         sent[0, j, i] = value.astype(BF16)
     pl.semaphore_wait(barrier, len(sides))
-    for i, j in EVEN + ODD:
+    for i, j in NODES:
         announce(0, i, j)
     tell(0)
     loads[2].wait()
@@ -327,7 +321,7 @@
     both = whole_shrink * extra
     ratio = whole_shrink / shrink
     rows = [None] * 3
-    for i, j in EVEN + ODD:
+    for i, j in NODES:
         land(3, i, j)
         unit_q = outer(3, i, j) * both
         for term, other in enumerate((scaled_w[i, j], unit_q, scaled_v[i, j])):

time: 38.4 us -> 38.4 us (level)
  no operation moved by 1% of the time
where the time goes in v7:
time: 38.4 us; the launch traced here: 38.3 us
  Pallas kernels  37.5 us (98%)
  local copies, waits for them, and re-layouts  0.75 us (2%)
    pallas_call x1, Pallas kernels, local(): pl.pallas_call(functools.partial(kernel, ngx, ngy, fast), out_shape=jax.S...  37.5 us

profile of v7, /device:TPU:1, one launch (start us, length us, event | category | flops | bytes accessed | tf_op | source)
XLA Modules:
  0.0 38.3 jit_solution(4175916864298333615)
XLA Ops:
  0.0 37.5 %shard_map.28 = f32[2,2,192,128]{3,2,1,0:T(8,128)S(1)} custom-call(f32[2,2,192,128]{3,2,1,0:T(8,128)} %load_ref.1, bf16[4,2,2,192,192]{4,3,2,1,0:T(8,128)(2,1)} %blocks_ref.1), custom_call_target="tpu_custom_call" | custom-call | tf_op jit(solution)/shard_map/pallas_call | solution.py:385
  37.6 0.7 %copy.4 = f32[2,2,192,128]{3,2,1,0:T(8,128)} copy(f32[2,2,192,128]{3,2,1,0:T(8,128)S(1)} %shard_map.28) | data formatting | bytes 786432

commit v8 on v6

--- a/solution.py
+++ b/solution.py
@@ -15,7 +15,7 @@
 PAIRS = [[[(0, 0)], [(1, 0)], [(0, 1)], [(1, 1)]]] * 5
 XL, XH, YL, YH = range(4)
 SLOTS = [(XL, 0), (XL, 1), (XH, 0), (XH, 1), (YL, None), (YH, None)]
-TERMS = 4
+TERMS = 3
 
 
 def dot(a, b):
@@ -259,7 +259,6 @@
         def _():
             halo[side] = jnp.zeros(halo.shape[1:], BF16)
 
-    mine[...] = jnp.zeros(mine.shape, F32)
 
     loads[0].wait()
     loads[1].wait()
@@ -357,7 +356,7 @@
     factors = []
     for k in range(len(theirs)):
         row = once[k : k + 1]
-        factors.append(jnp.concatenate([row, twice[k : k + 1], row, row], axis=0))
+        factors.append(jnp.concatenate([row, twice[k : k + 1], row], axis=0))
 
     last = functools.reduce(jnp.add, [factor * part for factor, part in zip(factors, arrive(1, 1))])
     wq, qq, bq = last[0:1], last[1:2], last[2:3]

time: 38.4 us -> 38.3 us (level)
  no operation moved by 1% of the time
where the time goes in v8:
time: 38.3 us
  Pallas kernels  37.5 us (98%)
  local copies, waits for them, and re-layouts  0.75 us (2%)
    pallas_call x1, Pallas kernels, local(): pl.pallas_call(functools.partial(kernel, ngx, ngy, fast), out_shape=jax.S...  37.5 us

profile of v8, /device:TPU:1, one launch (start us, length us, event | category | flops | bytes accessed | tf_op | source)
XLA Modules:
  0.0 38.3 jit_solution(9158094738142161303)
XLA Ops:
  0.0 37.5 %shard_map.28 = f32[2,2,192,128]{3,2,1,0:T(8,128)S(1)} custom-call(f32[2,2,192,128]{3,2,1,0:T(8,128)} %load_ref.1, bf16[4,2,2,192,192]{4,3,2,1,0:T(8,128)(2,1)} %blocks_ref.1), custom_call_target="tpu_custom_call" | custom-call | tf_op jit(solution)/shard_map/pallas_call | solution.py:390
  37.5 0.7 %copy.4 = f32[2,2,192,128]{3,2,1,0:T(8,128)} copy(f32[2,2,192,128]{3,2,1,0:T(8,128)S(1)} %shard_map.28) | data formatting | bytes 786432
